TPU v7x, 32 devices: a whole 2x2x4 slice. The times are simulated.
32 devices in a mesh: section: 4 (over y, core), fsdp: 8 (over z, x).
Axes of the slice: x: 2, y: 2, z: 4, core: 2. Of those that a mesh axis runs over, the one named last changes fastest.
Arguments:
- layer_input: bfloat16 [4, 4096, 2048], P('section', 'fsdp'), may hold values from -6 to 6
- resid_grad: bfloat16 [4, 4096, 2048], P('section', 'fsdp'), may hold values from -6 to 6
- qkv_grad: bfloat16 [4, 4096, 3072], P('section', 'fsdp'), may hold values from -6 to 6
- prev_input: bfloat16 [4, 4096, 2048], P('section', 'fsdp'), may hold values from -6 to 6
- prev_qkv_grad: bfloat16 [4, 4096, 3072], P('section', 'fsdp'), may hold values from -0.059814453 to 0.059814453
- qkv_weight: bfloat16 [4, 2048, 3072], P('section', 'fsdp'), may hold values from -0.125 to 0.125
- norm_gain: float32 [4, 2048], P('section'), may hold values from 0.1 to 1.9
Outputs:
- upstream_grad: bfloat16 [4, 4096, 2048], P('section', 'fsdp')
- weight_grad: float32 [4, 2048, 3072], P('section', 'fsdp')
- gain_grad: float32 [4, 2048], P('section')
All inputs are finite; a program needn't handle non-finite values.
Results may differ from a plain program's by a relative error of at most 0.018.
Values may be sent and summed in bfloat16 or wider, within the bound.
No kernel may reach another device: no remote copies, remote signals or barrier semaphores. Data moves between devices by JAX's collectives and lax.ppermute only.
A program may use at most 128 MiB of HBM per device.

v0:
```python
import jax
import jax.numpy as jnp
from jax import lax
from jax.sharding import PartitionSpec as P

EPS = 1e-05


def from_behind(block, axis, distance):
    devices = range(lax.axis_size(axis))
    route = [(i - distance, i) for i in devices if i - distance in devices]
    return lax.ppermute(block, axis, route)


def row_scale(rows):
    values = rows.astype(jnp.float32)
    return lax.rsqrt(jnp.mean(values * values, axis=-1, keepdims=True) + EPS)


def transpose_product(grads, piece):
    return lax.dot_general(
        grads, piece, (((1,), (1,)), ((), ())), preferred_element_type=jnp.float32
    )


def local(layer_input, resid_grad, qkv_grad, prev_input, prev_qkv_grad, qkv_weight, norm_gain):
    rows_now = layer_input[0]
    grads_now = qkv_grad[0]
    rows_prev = prev_input[0]
    grads_prev = prev_qkv_grad[0]
    weight_rows = qkv_weight[0]
    gain = norm_gain[0]
    owned = weight_rows.shape[0]
    prev_scale = row_scale(rows_prev)
    prev_normed = (rows_prev.astype(jnp.float32) * prev_scale * gain[None, :]).astype(jnp.bfloat16)
    direction = transpose_product(
        grads_now, lax.all_gather(weight_rows, "fsdp", axis=0, tiled=True)
    )
    scale = row_scale(rows_now)
    values = rows_now.astype(jnp.float32)
    gained = gain[None, :] * direction
    inner = jnp.mean(gained * values, axis=-1, keepdims=True)
    local_grad = (
        resid_grad[0].astype(jnp.float32) + scale * gained - values * scale * scale * scale * inner
    ).astype(jnp.bfloat16)
    upstream_grad = from_behind(local_grad, "section", -1)
    upstream_grad, ready_rows = lax.optimization_barrier((upstream_grad, prev_normed))
    weight_grad = lax.psum_scatter(
        lax.dot_general(
            ready_rows, grads_prev, (((0,), (0,)), ((), ())), preferred_element_type=jnp.float32
        ).astype(jnp.bfloat16),
        "fsdp",
        scatter_dimension=0,
        tiled=True,
    ).astype(jnp.float32)
    owned_gain = lax.dynamic_slice_in_dim(gain, lax.axis_index("fsdp") * owned, owned, 0)
    gain_part = jnp.sum(weight_rows.astype(jnp.float32) * weight_grad, axis=1) / owned_gain
    gain_grad = lax.all_gather(gain_part, "fsdp", axis=0, tiled=True)
    return (upstream_grad[None], weight_grad[None], gain_grad[None])


def solution(mesh):
    placed = (
        P("section", "fsdp", None),
        P("section", "fsdp", None),
        P("section", "fsdp", None),
        P("section", "fsdp", None),
        P("section", "fsdp", None),
        P("section", "fsdp", None),
        P("section", None),
    )
    return jax.shard_map(
        local,
        mesh=mesh,
        in_specs=placed,
        out_specs=(P("section", "fsdp", None), P("section", "fsdp", None), P("section", None)),
        check_vma=False,
    )
```

profile of v0, /device:TPU:0, one launch (start us, length us, event | category | flops | bytes accessed | tf_op | source)
XLA Modules:
  0.0 485.1 jit_solution(3610837498675808142)
XLA Ops:
  7.2 0.0 copy-start
  7.2 0.0 copy-start.2
  7.2 0.0 all-gather.4.cloned.1.call-start
  7.2 0.7 all-gather.4.cloned.1.call-update
  7.9 0.0 reduce-scatter.2.cloned.1.call-start
  8.0 2.2 fusion.2
  10.2 179.2 %all-gather.4.cloned.1.call-done = bf16[1,2048,3072]{2,1,0:T(8,128)(2,1)} async-done(((bf16[1,256,3072]{2,1,0:T(8,128)(2,1)}), bf16[1,2048,3072]{2,1,0:T(8,128)(2,1)}) %all-gather.4.cloned.1.call-update) | async-done | bytes 12582928 | tf_op jit(solution)/shard_map/all_gather | solution.py:37
  189.4 0.0 copy-done.2
  189.4 15.1 %fusion.5 = (f32[512]{0:T(512)S(1)}, f32[512]{0:T(512)S(1)}, bf16[512,2048]{1,0:T(8,128)(2,1)}, f32[512,2048]{1,0:T(8,128)}) fusion(bf16[1,512,2048]{2,1,0:T(8,128)(2,1)} %param.7, f32[2048]{0:T(1024)S(1)} %bitcast.37, f32[512]{0:T(512)S(1)} %add_rsqrt_fusion, bf16[1,512,2048]{2,1,0:T(8,128)(2,1)} %param.10, ...), kind=kOutput, calls=%fused_computation.11 | convolution fusion | flops 6452935680 | bytes 26228736 | tf_op jit(solution)/shard_map/dot_general | solution.py:21
  204.5 0.0 copy-start.3
  204.5 5.3 %fusion.10 = bf16[512,2048]{1,0:T(8,128)(2,1)S(1)} fusion(f32[512,2048]{1,0:T(8,128)} %get-tuple-element.10, bf16[1,512,2048]{2,1,0:T(8,128)(2,1)} %param.8, bf16[1,512,2048]{2,1,0:T(8,128)(2,1)} %param.7, f32[512]{0:T(512)S(1)} %get-tuple-element.12, f32[2048]{0:T(1024)S(1)} %bitcast.38, f32[512]{0:T(512)S(1)} %get-tuple-element.11), kind=kLoop, calls=%fused_computation.16 | loop fusion | flops 11534336 | bytes 10498048 | tf_op jit(solution)/shard_map/convert_element_type | solution.py:45
  209.8 1.3 collective-permute-start
  211.1 4.9 %collective-permute-done = bf16[512,2048]{1,0:T(8,128)(2,1)} collective-permute-done((bf16[512,2048]{1,0:T(8,128)(2,1)S(1)}, bf16[512,2048]{1,0:T(8,128)(2,1)}, u32[]{:S(2)}, u32[]{:S(2)}) %collective-permute-start) | collective-permute-done | bytes 2097184 | tf_op jit(solution)/shard_map/ppermute | solution.py:12
  216.0 0.0 copy-done
  216.0 0.0 copy-done.3
  216.0 9.7 %convolution_convert_fusion = bf16[2048,3072]{1,0:T(8,128)(2,1)} fusion(bf16[512,2048]{1,0:T(8,128)(2,1)S(1)} %copy-done.3, bf16[1,512,3072]{2,1,0:T(8,128)(2,1)S(1)} %copy-done), kind=kOutput, calls=%fused_computation.2 | convolution fusion | flops 6448742400 | bytes 17825792 | tf_op jit(solution)/shard_map/dot_general | solution.py:49
  225.7 0.0 reduce-scatter.2.cloned.1.call-update
  225.7 225.6 %reduce-scatter.2.cloned.1.call-done = bf16[256,3072]{1,0:T(8,128)(2,1)} async-done(((bf16[2048,3072]{1,0:T(8,128)(2,1)}), bf16[256,3072]{1,0:T(8,128)(2,1)}) %reduce-scatter.2.cloned.1.call-update) | async-done | bytes 1572880 | tf_op jit(solution)/shard_map/reduce_scatter | solution.py:48
  451.4 0.0 copy-start.1
  451.4 2.5 fusion.12
  453.9 18.6 %all-gather.1 = f32[8,1,256]{2,1,0:T(1,128)S(1)} all-gather(f32[1,1,256]{2,1,0:T(1,128)S(1)} %bitcast.39), channel_id=1, replica_groups=mesh['section'=4,'fsdp'=8] {'fsdp'}, dimensions={0}, use_global_device_ids=true | all-gather | bytes 9216 | tf_op jit(solution)/shard_map/all_gather | solution.py:58
  472.4 0.0 copy-done.1
  472.4 2.0 convert_bitcast_fusion
  474.5 3.2 copy.12
  477.6 0.6 copy.13
  (4 shorter events, 0.0 us)
Async XLA Ops:
  7.2 208.8 %copy-start = (bf16[1,512,3072]{2,1,0:T(8,128)(2,1)S(1)}, bf16[1,512,3072]{2,1,0:T(8,128)(2,1)}, u32[]{:S(2)}) copy-start(bf16[1,512,3072]{2,1,0:T(8,128)(2,1)} %param.11) | copy-start | bytes 9437188
  7.2 182.2 %copy-start.2 = (f32[1,2048]{1,0:T(1,128)S(1)}, f32[1,2048]{1,0:T(1,128)}, u32[]{:S(2)}) copy-start(f32[1,2048]{1,0:T(1,128)} %param.13) | copy-start | bytes 24580
  7.2 182.2 %all-gather.4.cloned.1.call-start = ((), (), s32[]{:S(2)}) async-start(), calls=%async_computation.2 | async-start | bytes 14155776 | tf_op jit(solution)/shard_map/all_gather | solution.py:37
  7.9 443.4 %reduce-scatter.2.cloned.1.call-start = ((), (), s32[]{:S(2)}) async-start(), calls=%async_computation.1 | async-start | bytes 14155776 | tf_op jit(solution)/shard_map/reduce_scatter | solution.py:48
  204.5 11.5 %copy-start.3 = (bf16[512,2048]{1,0:T(8,128)(2,1)S(1)}, bf16[512,2048]{1,0:T(8,128)(2,1)}, u32[]{:S(2)}) copy-start(bf16[512,2048]{1,0:T(8,128)(2,1)} %get-tuple-element.6) | copy-start | bytes 6291460
  209.8 6.2 %collective-permute-start = (bf16[512,2048]{1,0:T(8,128)(2,1)S(1)}, bf16[512,2048]{1,0:T(8,128)(2,1)}, u32[]{:S(2)}, u32[]{:S(2)}) collective-permute-start(bf16[512,2048]{1,0:T(8,128)(2,1)S(1)} %fusion.10), channel_id=1, source_target_pairs={{8,0},{16,8},{24,16},{9,1},{17,9},{25,17},{10,2},{18,10},{26,18},{... | collective-permute-start | bytes 6291464 | tf_op jit(solution)/shard_map/ppermute | solution.py:12
  451.4 21.1 %copy-start.1 = (bf16[256,3072]{1,0:T(8,128)(2,1)S(1)}, bf16[256,3072]{1,0:T(8,128)(2,1)}, u32[]{:S(2)}) copy-start(bf16[256,3072]{1,0:T(8,128)(2,1)} %reduce-scatter.2.cloned.1.call-done) | copy-start | bytes 4718596
Sparse Core Ops, SparseCore 0:
  10.2 179.1 all-gather.3
  225.8 225.4 reduce-scatter.1
where the time goes:
time: 485 us
  waiting for transfers between devices  410 us (85%)
  matrix products  24.8 us (5%)
  blocking collectives  18.6 us (4%)
  between operations  14.1 us (3%)
  other arithmetic  12 us (2%)
    reduce_scatter x1, waiting for transfers between devices, local(): lax.psum_scatter(lax.dot_general(ready_rows, grads_prev, (((0,), (0,)), (...  226 us
    all_gather x1, waiting for transfers between devices, local(): lax.all_gather(weight_rows, 'fsdp', axis=0, tiled=True)  179 us
    all_gather x1, blocking collectives, local(): gain_grad = lax.all_gather(gain_part, 'fsdp', axis=0, tiled=True)  18.6 us
    dot_general x1, matrix products, transpose_product(): lax.dot_general(grads, piece, (((1,), (1,)), ((), ())), preferred_element...  15.1 us
    dot_general x1, matrix products, local(): lax.dot_general(ready_rows, grads_prev, (((0,), (0,)), ((), ())), preferr...  9.72 us
  transfers between devices with their start and end apart: 3, of which 3 were waited for; matrix products, arithmetic and copies ran while one was open for 0% of the time, Pallas kernels for 0%

commit v1 on v0

v1 whole, which is shorter than its diff:
```python
import math

import jax
import jax.numpy as jnp
from jax import lax
from jax.experimental import pallas as pl
from jax.experimental.pallas import tpu as pltpu
from jax.sharding import PartitionSpec as P

EPS = 1e-05
BF16 = jnp.bfloat16
F32 = jnp.float32


def row_scale(rows):
    values = rows.astype(F32)
    return lax.rsqrt(jnp.mean(values * values, axis=-1, keepdims=True) + EPS)


def swap(value, axis):
    count = lax.axis_size(axis)
    return lax.ppermute(value, axis, [(i, i ^ 1) for i in range(count)])


def hop(value, axis, sources, step):
    return lax.ppermute(
        value, axis, [(2 * o + q, 2 * (o + step) + q) for o in sources for q in range(2)]
    )


def split_halves(array, owned):
    pieces = [array[..., i : i + owned] for i in range(0, array.shape[-1], owned)]
    return jnp.concatenate(pieces[0::2], axis=-1), jnp.concatenate(pieces[1::2], axis=-1)


def join_halves(even, odd, owned):
    pieces = []
    for i in range(0, even.shape[-1], owned):
        pieces += [even[..., i : i + owned], odd[..., i : i + owned]]
    return jnp.concatenate(pieces, axis=-1)


class Gather:
    def __init__(self, shard, axis, pairs, pair):
        self.shard, self.axis, self.pairs, self.pair = shard, axis, pairs, pair
        self.ups, self.downs, self.flying = [], [], []
        self.advance()

    def advance(self):
        if self.flying:
            self.ups.append(self.flying[0])
            self.downs.append(self.flying[1])
        r = len(self.ups) + 1
        up = hop(([self.shard] + self.ups)[-1], self.axis, range(r - 1, self.pairs - 1), 1)
        down = hop(([self.shard] + self.downs)[-1], self.axis, range(1, self.pairs - r + 1), -1)
        self.flying = [up, down]

    def done(self):
        return len(self.ups) == self.pairs - 2

    def whole(self):
        return assemble(self.pair, self.shard, self.ups + self.flying[:1], self.downs + self.flying[1:])


class Scatter:
    def __init__(self, term, axis, pairs, pair, owned):
        self.term, self.axis, self.pairs, self.pair, self.owned = term, axis, pairs, pair, owned
        self.step, self.flying = 0, []
        self.advance()

    def advance(self):
        self.step += 1
        s, pairs, pair = self.step, self.pairs, self.pair
        above = jnp.minimum(pair + pairs - s, pairs - 1)
        below = jnp.maximum(pair - pairs + s, 0)
        if s == 1 and pairs >= 4:
            (send,) = pick_and_add(self.term, [jnp.where(pair < pairs // 2, above, below)], [], self.owned)
            route = [(q, 2 + q) for q in range(2)]
            route += [(2 * pairs - 2 + q, 2 * pairs - 4 + q) for q in range(2)]
            self.flying = [lax.ppermute(send, self.axis, route)]
            return
        came = [self.flying[0], self.flying[-1]] if self.flying else []
        send_up, send_down = pick_and_add(self.term, [above, below], came, self.owned)
        self.flying = [
            hop(send_up, self.axis, range(s), 1),
            hop(send_down, self.axis, range(pairs - s, pairs), -1),
        ]

    def done(self):
        return self.step == self.pairs - 1

    def total(self):
        own = lax.dynamic_slice_in_dim(self.term, self.pair * self.owned, self.owned, 0)
        return own.astype(F32) + sum(came.astype(F32) for came in self.flying)


SMALL = pl.CostEstimate(flops=1, bytes_accessed=1, transcendentals=0)
PARAMS = pltpu.CompilerParams(vmem_limit_bytes=48 * 1024 * 1024)


def assemble(pair, shard, ups, downs):
    pairs, owned = len(ups) + 1, shard.shape[0]

    def kernel(pair_ref, shard_ref, *refs):
        up_refs, down_refs = refs[: pairs - 1], refs[pairs - 1 : 2 * pairs - 2]
        out_ref, slots, came, gone = refs[2 * pairs - 2 :]
        here = pair_ref[0]

        def bring(source, at):
            return pltpu.make_async_copy(source, slots.at[at], came.at[at])

        def put(at):
            return pltpu.make_async_copy(slots.at[at], out_ref.at[pl.ds(at * owned, owned)], gone.at[at])

        for at in range(pairs):
            for source_pair in range(pairs):
                distance = source_pair - at
                if distance == 0:
                    source = shard_ref
                elif distance > 0:
                    source = up_refs[distance - 1]
                else:
                    source = down_refs[-distance - 1]

                @pl.when(here == source_pair)
                def _(source=source, at=at):
                    bring(source, at).start()

        for at in range(pairs):
            bring(shard_ref, at).wait()
            put(at).start()
        for at in range(pairs):
            put(at).wait()

    return pl.pallas_call(
        kernel,
        out_shape=jax.ShapeDtypeStruct((pairs * owned, shard.shape[1]), shard.dtype),
        in_specs=[pl.BlockSpec(memory_space=pltpu.SMEM)] + [pl.BlockSpec(memory_space=pl.ANY)] * (2 * pairs - 1),
        out_specs=pl.BlockSpec(memory_space=pl.ANY),
        scratch_shapes=[
            pltpu.VMEM((pairs,) + shard.shape, shard.dtype),
            pltpu.SemaphoreType.DMA((pairs,)),
            pltpu.SemaphoreType.DMA((pairs,)),
        ],
        compiler_params=PARAMS,
        cost_estimate=SMALL,
    )(pair.reshape(1), shard, *ups, *downs)


def first_packet(rows, gain, grads, wide, side, owned):
    tokens, features = rows.shape
    half = features // 2
    block = min(128, tokens)

    def kernel(side_ref, rows_ref, gain_ref, grads_ref, mine_ref, packet_ref):
        values = rows_ref[...].astype(F32)
        scale = lax.rsqrt(jnp.mean(values * values, axis=-1, keepdims=True) + EPS)
        normed = (values * scale * gain_ref[...]).astype(BF16)
        even, odd = split_halves(normed, owned)
        packet_ref[:, half:] = grads_ref[...]

        @pl.when(side_ref[0] == 0)
        def _():
            mine_ref[...] = even.T
            packet_ref[:, :half] = odd

        @pl.when(side_ref[0] != 0)
        def _():
            mine_ref[...] = odd.T
            packet_ref[:, :half] = even

    return pl.pallas_call(
        kernel,
        grid=(tokens // block,),
        in_specs=[
            pl.BlockSpec(memory_space=pltpu.SMEM),
            pl.BlockSpec((block, features), lambda i: (i, 0)),
            pl.BlockSpec((1, features), lambda i: (0, 0)),
            pl.BlockSpec((block, wide), lambda i: (i, 0)),
        ],
        out_specs=[
            pl.BlockSpec((half, block), lambda i: (0, i)),
            pl.BlockSpec((block, half + wide), lambda i: (i, 0)),
        ],
        out_shape=[
            jax.ShapeDtypeStruct((half, tokens), BF16),
            jax.ShapeDtypeStruct((tokens, half + wide), BF16),
        ],
        compiler_params=PARAMS,
        cost_estimate=SMALL,
    )(side.reshape(1), rows, gain[None, :], grads)


def pick_and_add(term, places, came, owned):
    wide = term.shape[1]
    block = wide // 2
    count = len(places)

    def kernel(at_ref, *refs):
        for i in range(count):
            value = refs[i][...]
            if came:
                value = (value.astype(F32) + refs[count + i][...].astype(F32)).astype(BF16)
            refs[-count + i][...] = value

    plain = pl.BlockSpec((owned, block), lambda j, at: (0, j))
    return pl.pallas_call(
        kernel,
        grid_spec=pltpu.PrefetchScalarGridSpec(
            num_scalar_prefetch=1,
            grid=(wide // block,),
            in_specs=[
                pl.BlockSpec((owned, block), lambda j, at, i=i: (at[i], j)) for i in range(count)
            ] + [plain] * len(came),
            out_specs=[plain] * count,
        ),
        out_shape=[jax.ShapeDtypeStruct((owned, wide), BF16)] * count,
        compiler_params=PARAMS,
        cost_estimate=SMALL,
    )(jnp.stack(places), *[term] * count, *came)


def transpose_product(grads, weight, dtype):
    rows, depth = grads.shape
    block = min(256, weight.shape[0])

    def kernel(grads_ref, weight_ref, out_ref, flipped):
        @pl.when(pl.program_id(0) == 0)
        def _():
            flipped[...] = grads_ref[...].T

        product = jnp.dot(weight_ref[...], flipped[...], preferred_element_type=F32)
        out_ref[...] = product.T.astype(dtype)

    return pl.pallas_call(
        kernel,
        grid=(weight.shape[0] // block,),
        in_specs=[
            pl.BlockSpec((rows, depth), lambda j: (0, 0)),
            pl.BlockSpec((block, depth), lambda j: (j, 0)),
        ],
        out_specs=pl.BlockSpec((rows, block), lambda j: (0, j)),
        out_shape=jax.ShapeDtypeStruct((rows, weight.shape[0]), dtype),
        scratch_shapes=[pltpu.VMEM((depth, rows), grads.dtype)],
        compiler_params=PARAMS,
        cost_estimate=SMALL,
    )(grads, weight)


def input_gradient(mine, theirs, start, rows, resid, gain, side, owned):
    tokens, half = theirs.shape
    features = 2 * half
    block = min(128, tokens)
    first_block = start // block

    def kernel(side_ref, mine_ref, theirs_ref, rows_ref, resid_ref, gain_ref, out_ref):
        def result(even, odd):
            values = rows_ref[...].astype(F32)
            scale = lax.rsqrt(jnp.mean(values * values, axis=-1, keepdims=True) + EPS)
            gained = gain_ref[...] * join_halves(even, odd, owned)
            inner = jnp.mean(gained * values, axis=-1, keepdims=True)
            out_ref[...] = (
                resid_ref[...].astype(F32) + scale * gained - values * (scale * scale * scale * inner)
            ).astype(BF16)

        @pl.when(side_ref[0] == 0)
        def _():
            result(mine_ref[...], theirs_ref[...].astype(F32))

        @pl.when(side_ref[0] != 0)
        def _():
            result(theirs_ref[...].astype(F32), mine_ref[...])

    return pl.pallas_call(
        kernel,
        grid=(tokens // block,),
        in_specs=[
            pl.BlockSpec(memory_space=pltpu.SMEM),
            pl.BlockSpec((block, half), lambda i: (first_block + i, 0)),
            pl.BlockSpec((block, half), lambda i: (i, 0)),
            pl.BlockSpec((block, features), lambda i: (first_block + i, 0)),
            pl.BlockSpec((block, features), lambda i: (first_block + i, 0)),
            pl.BlockSpec((1, features), lambda i: (0, 0)),
        ],
        out_specs=pl.BlockSpec((block, features), lambda i: (i, 0)),
        out_shape=jax.ShapeDtypeStruct((tokens, features), BF16),
        compiler_params=PARAMS,
        cost_estimate=SMALL,
    )(side.reshape(1), mine, theirs, rows, resid, gain[None, :])


def weight_term(mine, grads, start, packet, got, got_start):
    features, tokens = mine.shape
    wide = got.shape[1] - got_start
    block = math.gcd(math.gcd(start, wide), math.gcd(got_start, 512))
    first_block, first_got = start // block, got_start // block

    def kernel(mine_ref, grads_ref, theirs_ref, got_ref, out_ref, flipped):
        @pl.when(pl.program_id(0) == 0)
        def _():
            flipped[...] = theirs_ref[...].T

        total = jnp.dot(mine_ref[...], grads_ref[...], preferred_element_type=F32)
        total += jnp.dot(flipped[...], got_ref[...], preferred_element_type=F32)
        out_ref[...] = total.astype(BF16)

    return pl.pallas_call(
        kernel,
        grid=(wide // block,),
        in_specs=[
            pl.BlockSpec((features, tokens), lambda j: (0, 0)),
            pl.BlockSpec((tokens, block), lambda j: (0, first_block + j)),
            pl.BlockSpec((tokens, features), lambda j: (0, 0)),
            pl.BlockSpec((tokens, block), lambda j: (0, first_got + j)),
        ],
        out_specs=pl.BlockSpec((features, block), lambda j: (0, j)),
        out_shape=jax.ShapeDtypeStruct((features, wide), BF16),
        scratch_shapes=[pltpu.VMEM((features, tokens), BF16)],
        compiler_params=PARAMS,
        cost_estimate=SMALL,
    )(mine, grads, packet, got)


def swap_in(part, distance, axis):
    theirs = lax.ppermute(part, axis, [(i, i ^ distance) for i in range(lax.axis_size(axis))])
    low = lax.rem(lax.axis_index(axis) // distance, 2) == 0
    return jnp.where(low, jnp.concatenate([part, theirs]), jnp.concatenate([theirs, part]))


class Line:
    def __init__(self, token):
        self.token = token

    def arrived(self, *values):
        *values, self.token = lax.optimization_barrier((*values, self.token))
        return values if len(values) > 1 else values[0]

    def meet(self, chains, *values):
        flat = [array for chain in chains for array in chain.flying]
        flat = lax.optimization_barrier((*flat, *values, self.token))
        at = 0
        for chain in chains:
            chain.flying = list(flat[at : at + len(chain.flying)])
            at += len(chain.flying)
        self.token = flat[-1]
        return flat[at:-1]


def local(layer_input, resid_grad, qkv_grad, prev_input, prev_qkv_grad, qkv_weight, norm_gain):
    axis = "fsdp"
    rows_now, resid, grads_now = layer_input[0], resid_grad[0], qkv_grad[0]
    rows_prev, grads_prev = prev_input[0], prev_qkv_grad[0]
    weight_rows, gain = qkv_weight[0], norm_gain[0]
    owned, columns = weight_rows.shape
    tokens = rows_now.shape[0]
    count = lax.axis_size(axis)
    pairs = count // 2
    me = lax.axis_index(axis)
    pair, side = me // 2, lax.rem(me, 2)
    first = side == 0
    layers = lax.axis_size("section")
    line = Line(gain)

    cuts = [0, columns // 2, columns]
    bounds = [0, tokens // 2, tokens]
    parts = [slice(bounds[i], bounds[i + 1]) for i in range(2)]

    def summing(i, got, got_start):
        term = weight_term(normed_mine, grads_prev, cuts[i], packet, got, got_start)
        return Scatter(term, axis, pairs, pair, owned)

    def toward(got):
        return transpose_product(got, weight_half, BF16)

    def up_a_layer(i, theirs):
        local_grad = input_gradient(
            direction_mine, theirs, bounds[i], rows_now, resid, line.token, side, owned
        )
        return lax.ppermute(local_grad, "section", [(k + 1, k) for k in range(layers - 1)])

    normed_mine, packet = first_packet(rows_prev, gain, grads_prev, cuts[1], side, owned)
    packet = swap(line.arrived(packet), axis)
    gather = Gather(line.arrived(weight_rows), axis, pairs, pair)
    x2 = swap(line.arrived(grads_prev)[:, cuts[1] :], axis)

    line.meet([gather])
    gather.advance()
    (packet,) = line.meet([], packet)
    sum0 = summing(0, packet, normed_mine.shape[0])
    g0 = swap(line.arrived(grads_now[parts[0]]), axis)
    line.meet([gather])
    gather.advance()
    line.meet([sum0])
    sum0.advance()
    g1 = swap(line.arrived(grads_now[parts[1]]), axis)
    (x2,) = line.meet([], x2)
    sum1 = summing(1, x2, 0)
    line.meet([sum0])
    sum0.advance()
    line.meet([gather])
    while not gather.done():
        gather.advance()
        line.meet([gather])
    weight_half = line.arrived(gather.whole())
    line.meet([sum1])
    sum1.advance()
    (g0,) = line.meet([], g0)
    r0 = swap(line.arrived(toward(g0)), axis)
    direction_mine = line.arrived(transpose_product(grads_now, weight_half, F32))
    line.meet([sum1])
    sum1.advance()
    (g1,) = line.meet([], g1)
    r1 = swap(line.arrived(toward(g1)), axis)
    r0 = line.arrived(r0)
    u0 = up_a_layer(0, r0)
    line.meet([sum0, sum1])
    for chain in (sum0, sum1):
        while not chain.done():
            chain.advance()
            line.meet([chain])
    weight_grad = jnp.concatenate([chain.total() for chain in (sum0, sum1)], axis=1)
    owned_gain = lax.dynamic_slice_in_dim(gain, me * owned, owned, 0)
    gain_part = jnp.sum(weight_rows.astype(F32) * weight_grad, axis=1) / owned_gain
    gain_grad = swap_in(gain_part, 1, axis)
    r1 = line.arrived(r1)
    u1 = up_a_layer(1, r1)
    distance = 2
    while distance < count:
        gain_grad = swap_in(gain_grad, distance, axis)
        distance *= 2
    upstream_grad = jnp.concatenate([u0, u1], axis=0)
    return (upstream_grad[None], weight_grad[None], gain_grad[None])


def solution(mesh):
    placed = (
        P("section", "fsdp", None),
        P("section", "fsdp", None),
        P("section", "fsdp", None),
        P("section", "fsdp", None),
        P("section", "fsdp", None),
        P("section", "fsdp", None),
        P("section", None),
    )
    return jax.shard_map(
        local,
        mesh=mesh,
        in_specs=placed,
        out_specs=(P("section", "fsdp", None), P("section", "fsdp", None), P("section", None)),
        check_vma=False,
    )
```

time: 485 us -> 225 us (0.46)
  waiting for transfers between devices: 410 us -> 82.9 us
  starting transfers between devices: 1.37 us -> 58.9 us
  Pallas kernels: 0 us -> 55.9 us
  matrix products: 24.8 us -> 0 us
  blocking collectives: 18.6 us -> 0 us
  between operations: 14.1 us -> 0.97 us
  local copies, waits for them, and re-layouts: 3.79 us -> 15.8 us
    reduce_scatter x1 -> x0, waiting for transfers between devices: 226 us -> none  [local(): lax.psum_scatter(lax.dot_general(ready_rows, grads_prev, (((0,), (0,)), (...]
    all_gather x1 -> x0, waiting for transfers between devices: 179 us -> none  [local(): lax.all_gather(weight_rows, 'fsdp', axis=0, tiled=True)]
    ppermute x1 -> x27, waiting for transfers between devices: 4.89 us -> 82.9 us  [the longest x14 62.1 us: hop(): lax.ppermute(value, axis, [(2 * o + q, 2 * (o + step) + q) for o in sourc...]
    ppermute x1 -> x27, starting transfers between devices: 1.29 us -> 58.9 us  [the longest x14 34.8 us: hop(): lax.ppermute(value, axis, [(2 * o + q, 2 * (o + step) + q) for o in sourc...]
    pallas_call x0 -> x15, Pallas kernels: none -> 55.9 us  [the longest x3 19.2 us: transpose_product(): pl.pallas_call(kernel, grid=(weight.shape[0] // block,), in_specs=[pl.Blo...]
    dot_general x2 -> x0, matrix products: 24.8 us -> none  [the longest x1 15.1 us: transpose_product(): lax.dot_general(grads, piece, (((1,), (1,)), ((), ())), preferred_element...]
    all_gather x1 -> x0, blocking collectives: 18.6 us -> none  [local(): gain_grad = lax.all_gather(gain_part, 'fsdp', axis=0, tiled=True)]
    unnamed x10 -> x38, local copies, waits for them, and re-layouts: 3.78 us -> 12.7 us
  transfers between devices with their start and end apart: 3 -> 27, of which waited for: 3 -> 12; matrix products, arithmetic and copies ran while one was open for 0% -> 4% of each run, Pallas kernels for 0% -> 23%
where the time goes in v1:
time: 225 us; the launch traced here: 224 us
  waiting for transfers between devices  82.9 us (37%)
  starting transfers between devices  58.9 us (26%)
  Pallas kernels  55.9 us (25%)
  local copies, waits for them, and re-layouts  15.8 us (7%)
  other arithmetic  9.35 us (4%)
    ppermute x14, waiting for transfers between devices, hop(): lax.ppermute(value, axis, [(2 * o + q, 2 * (o + step) + q) for o in sourc...  62.1 us
    ppermute x14, starting transfers between devices, hop(): lax.ppermute(value, axis, [(2 * o + q, 2 * (o + step) + q) for o in sourc...  34.8 us
    pallas_call x3, Pallas kernels, transpose_product(): pl.pallas_call(kernel, grid=(weight.shape[0] // block,), in_specs=[pl.Blo...  19.2 us
    pallas_call x2, Pallas kernels, weight_term(): pl.pallas_call(kernel, grid=(wide // block,), in_specs=[pl.BlockSpec((fea...  13 us
    unnamed x38, local copies, waits for them, and re-layouts  12.7 us
    ppermute x6, waiting for transfers between devices, swap(): return lax.ppermute(value, axis, [(i, i ^ 1) for i in range(count)])  11 us
    pallas_call x6, Pallas kernels, pick_and_add(): pl.pallas_call(kernel, grid_spec=pltpu.PrefetchScalarGridSpec(num_scalar_...  9.68 us
    ppermute x6, starting transfers between devices, swap(): return lax.ppermute(value, axis, [(i, i ^ 1) for i in range(count)])  9.39 us
  transfers between devices with their start and end apart: 27, of which 12 were waited for; matrix products, arithmetic and copies ran while one was open for 4% of the time, Pallas kernels for 23%

profile of v1, /device:TPU:0, one launch (start us, length us, event | category | flops | bytes accessed | tf_op | source)
XLA Modules:
  0.0 223.8 jit_solution(17105496201393704046)
XLA Ops:
  0.6 1.6 copy-done.11
  2.9 4.7 %shard_map.94 = (bf16[1024,512]{1,0:T(8,128)(2,1)S(1)}, bf16[512,2560]{1,0:T(8,128)(2,1)}) custom-call(s32[1]{0:T(128)} %bitcast.side_ref, bf16[512,2048]{1,0:T(8,128)(2,1)S(1)} %bitcast.34, f32[1,2048]{1,0:T(1,128)S(1)} %copy-done.16, bf16[512,3072]{1,0:T(8,128)(2,1)} %bitcast.35), custom_call_target="tpu_custom_call" | custom-call | flops 1 | bytes 1 | tf_op jit(solution)/shard_map/pallas_call | solution.py:172
  7.6 2.9 %collective-permute-start.4 = (bf16[512,2560]{1,0:T(8,128)(2,1)}, bf16[512,2560]{1,0:T(8,128)(2,1)S(1)}, u32[]{:S(2)}, u32[]{:S(2)}) collective-permute-start(bf16[512,2560]{1,0:T(8,128)(2,1)} %get-tuple-element.74), channel_id=1, source_target_pairs={{0,1},{1,0},{2,3},{3,2},{4,5},{5,4},{6,7},{7,6},{8,9},{9,8},{10,11... | collective-permute-start | bytes 7864328 | tf_op jit(solution)/shard_map/ppermute | solution.py:22
  10.5 4.6 %collective-permute-start = (bf16[256,3072]{1,0:T(8,128)(2,1)S(1)}, bf16[256,3072]{1,0:T(8,128)(2,1)}, u32[]{:S(2)}, u32[]{:S(2)}) collective-permute-start(bf16[256,3072]{1,0:T(8,128)(2,1)S(1)} %bitcast.31), channel_id=1, source_target_pairs={{0,2},{1,3},{2,4},{3,5},{4,6},{5,7},{8,10},{9,11},{10,12},{11,13},... | collective-permute-start | bytes 4718600 | tf_op jit(solution)/shard_map/ppermute | solution.py:26
  16.4 30.9 %collective-permute-done.refs_0_ = bf16[256,3072]{1,0:T(8,128)(2,1)} collective-permute-done((bf16[256,3072]{1,0:T(8,128)(2,1)S(1)}, bf16[256,3072]{1,0:T(8,128)(2,1)}, u32[]{:S(2)}, u32[]{:S(2)}) %collective-permute-start) | collective-permute-done | bytes 1572896 | tf_op jit(solution)/shard_map/ppermute | solution.py:26
  47.3 5.4 %collective-permute-done.1.refs_3_ = bf16[256,3072]{1,0:T(8,128)(2,1)} collective-permute-done((bf16[256,3072]{1,0:T(8,128)(2,1)S(1)}, bf16[256,3072]{1,0:T(8,128)(2,1)}, u32[]{:S(2)}, u32[]{:S(2)}) %collective-permute-start.1) | collective-permute-done | bytes 1572896 | tf_op jit(solution)/shard_map/ppermute | solution.py:26
  52.7 1.9 collective-permute-start.2
  57.7 10.7 %collective-permute-done.4.theirs_ref.got_ref = bf16[512,2560]{1,0:T(8,128)(2,1)S(1)} collective-permute-done((bf16[512,2560]{1,0:T(8,128)(2,1)}, bf16[512,2560]{1,0:T(8,128)(2,1)S(1)}, u32[]{:S(2)}, u32[]{:S(2)}) %collective-permute-start.4) | collective-permute-done | bytes 2621472 | tf_op jit(solution)/shard_map/ppermute | solution.py:22
  69.6 6.4 %shard_map.95.refs_0_.refs_1_ = bf16[1024,1536]{1,0:T(8,128)(2,1)} custom-call(bf16[1024,512]{1,0:T(8,128)(2,1)S(1)} %copy-done.9, bf16[512,3072]{1,0:T(8,128)(2,1)} %bitcast.36, bf16[512,2560]{1,0:T(8,128)(2,1)S(1)} %collective-permute-done.4.theirs_ref.got_ref, bf16[512,2560]{1,0:T(8,128)(2,1)S(1)} %collective-permute-done.4.theirs_ref.got_ref), custom_call_target="tpu_custom_call" | custom-call | flops 1 | bytes 1 | tf_op jit(solution)/shard_map/pallas_call | solution.py:307
  76.0 1.9 copy-done
  78.1 4.3 %collective-permute-start.7 = (bf16[256,1536]{1,0:T(8,128)(2,1)S(1)}, bf16[256,1536]{1,0:T(8,128)(2,1)S(1)}, u32[]{:S(2)}, u32[]{:S(2)}) collective-permute-start(bf16[256,1536]{1,0:T(8,128)(2,1)S(1)} %shard_map.96), channel_id=1, source_target_pairs={{0,2},{1,3},{6,4},{7,5},{8,10},{9,11},{14,12},{15,13},{16,18},{17,... | collective-permute-start | bytes 2359304 | tf_op jit(solution)/shard_map/ppermute | solution.py:80
  82.4 1.9 slice_bitcast_fusion
  84.3 8.4 %collective-permute-done.3.refs_4_ = bf16[256,3072]{1,0:T(8,128)(2,1)} collective-permute-done((bf16[256,3072]{1,0:T(8,128)(2,1)}, bf16[256,3072]{1,0:T(8,128)(2,1)}, u32[]{:S(2)}, u32[]{:S(2)}) %collective-permute-start.3) | collective-permute-done | bytes 1572896 | tf_op jit(solution)/shard_map/ppermute | solution.py:26
  92.7 1.8 collective-permute-start.5
  98.5 4.4 %collective-permute-start.8 = (bf16[256,1536]{1,0:T(8,128)(2,1)S(1)}, bf16[256,1536]{1,0:T(8,128)(2,1)S(1)}, u32[]{:S(2)}, u32[]{:S(2)}) collective-permute-start(bf16[256,1536]{1,0:T(8,128)(2,1)S(1)} %get-tuple-element.84), channel_id=1, source_target_pairs={{0,2},{1,3},{2,4},{3,5},{8,10},{9,11},{10,12},{11,13},{16,18},{17,... | collective-permute-start | bytes 2359304 | tf_op jit(solution)/shard_map/ppermute | solution.py:26
  103.7 1.5 collective-permute-start.11
  105.2 6.6 %shard_map.100.refs_0_.refs_1_ = bf16[1024,1536]{1,0:T(8,128)(2,1)} custom-call(bf16[1024,512]{1,0:T(8,128)(2,1)S(1)} %copy-done.10, bf16[512,3072]{1,0:T(8,128)(2,1)} %bitcast.37, bf16[512,2560]{1,0:T(8,128)(2,1)S(1)} %collective-permute-done.4.theirs_ref.got_ref, bf16[512,1536]{1,0:T(8,128)(2,1)} %collective-permute-done.10.got_ref), custom_call_target="tpu_custom_call" | custom-call | flops 1 | bytes 1 | tf_op jit(solution)/shard_map/pallas_call | solution.py:307
  111.8 1.9 copy-done.1
  113.9 3.1 %collective-permute-done.8.refs_2_ = bf16[256,1536]{1,0:T(8,128)(2,1)S(1)} collective-permute-done((bf16[256,1536]{1,0:T(8,128)(2,1)S(1)}, bf16[256,1536]{1,0:T(8,128)(2,1)S(1)}, u32[]{:S(2)}, u32[]{:S(2)}) %collective-permute-start.8) | collective-permute-done | bytes 786464 | tf_op jit(solution)/shard_map/ppermute | solution.py:26
  117.0 4.4 %collective-permute-start.12 = (bf16[256,1536]{1,0:T(8,128)(2,1)S(1)}, bf16[256,1536]{1,0:T(8,128)(2,1)S(1)}, u32[]{:S(2)}, u32[]{:S(2)}) collective-permute-start(bf16[256,1536]{1,0:T(8,128)(2,1)S(1)} %shard_map.101), channel_id=1, source_target_pairs={{0,2},{1,3},{6,4},{7,5},{8,10},{9,11},{14,12},{15,13},{16,18},{17,... | collective-permute-start | bytes 2359304 | tf_op jit(solution)/shard_map/ppermute | solution.py:80
  122.3 1.4 collective-permute-start.14
  123.8 6.6 %collective-permute-done.6.refs_5_ = bf16[256,3072]{1,0:T(8,128)(2,1)} collective-permute-done((bf16[256,3072]{1,0:T(8,128)(2,1)}, bf16[256,3072]{1,0:T(8,128)(2,1)}, u32[]{:S(2)}, u32[]{:S(2)}) %collective-permute-start.6) | collective-permute-done | bytes 1572896 | tf_op jit(solution)/shard_map/ppermute | solution.py:26
  130.4 4.6 %shard_map.98.weight_ref = bf16[1024,3072]{1,0:T(8,128)(2,1)} custom-call(s32[1]{0:T(128)} %bitcast.2.pair_ref, bf16[256,3072]{1,0:T(8,128)(2,1)S(1)} %bitcast.33, bf16[256,3072]{1,0:T(8,128)(2,1)} %collective-permute-done.refs_0_, bf16[256,3072]{1,0:T(8,128)(2,1)} %collective-permute-done.2.refs_1_, bf16[256,3072]{1,0:T(8,128)(2,1)} %collective-permute-done.5.refs_2_, ...), custom_call_target="tpu_custom_call" | custom-call | flops 1 | bytes 1 | tf_op jit(solution)/shard_map/pallas_call | solution.py:135
  136.0 2.0 shard_map.103
  138.0 3.1 %collective-permute-start.15 = (bf16[256,1536]{1,0:T(8,128)(2,1)}, bf16[256,1536]{1,0:T(8,128)(2,1)S(1)}, u32[]{:S(2)}, u32[]{:S(2)}) collective-permute-start(bf16[256,1536]{1,0:T(8,128)(2,1)} %get-tuple-element.106), channel_id=1, source_target_pairs={{0,2},{1,3},{2,4},{3,5},{8,10},{9,11},{10,12},{11,13},{16,18},{17,... | collective-permute-start | bytes 2359304 | tf_op jit(solution)/shard_map/ppermute | solution.py:26
  141.9 5.9 %shard_map.102 = bf16[256,1024]{1,0:T(8,128)(2,1)S(1)} custom-call(bf16[256,3072]{1,0:T(8,128)(2,1)} %collective-permute-done.11.grads_ref, bf16[1024,3072]{1,0:T(8,128)(2,1)} %shard_map.98.weight_ref), custom_call_target="tpu_custom_call" | custom-call | flops 1 | bytes 1 | tf_op jit(solution)/shard_map/pallas_call | solution.py:235
  147.8 1.5 collective-permute-start.13
  149.3 3.0 %shard_map.106 = (bf16[256,1536]{1,0:T(8,128)(2,1)}, bf16[256,1536]{1,0:T(8,128)(2,1)}) custom-call(s32[2]{0:T(128)S(1)} %get-tuple-element.136.at_ref, bf16[1024,1536]{1,0:T(8,128)(2,1)} %shard_map.95.refs_0_.refs_1_, bf16[1024,1536]{1,0:T(8,128)(2,1)} %shard_map.95.refs_0_.refs_1_, bf16[256,1536]{1,0:T(8,128)(2,1)S(1)} %collective-permute-done.8.refs_2_, ...), custom_call_target="tpu_custom_call" | custom-call | flops 1 | bytes 1 | tf_op jit(solution)/shard_map/pallas_call | solution.py:207
  152.3 5.4 %collective-permute-start.19 = (bf16[256,1536]{1,0:T(8,128)(2,1)}, bf16[256,1536]{1,0:T(8,128)(2,1)}, u32[]{:S(2)}, u32[]{:S(2)}) collective-permute-start(bf16[256,1536]{1,0:T(8,128)(2,1)} %get-tuple-element.118), channel_id=1, source_target_pairs={{0,2},{1,3},{2,4},{3,5},{4,6},{5,7},{8,10},{9,11},{10,12},{11,13},... | collective-permute-start | bytes 2359304 | tf_op jit(solution)/shard_map/ppermute | solution.py:26
  157.7 7.2 %shard_map.99.mine_ref = f32[512,1024]{1,0:T(8,128)S(1)} custom-call(bf16[512,3072]{1,0:T(8,128)(2,1)S(1)} %bitcast.28, bf16[1024,3072]{1,0:T(8,128)(2,1)} %shard_map.98.weight_ref), custom_call_target="tpu_custom_call" | custom-call | flops 1 | bytes 1 | tf_op jit(solution)/shard_map/pallas_call | solution.py:235
  166.3 3.0 %shard_map.107 = (bf16[256,1536]{1,0:T(8,128)(2,1)}, bf16[256,1536]{1,0:T(8,128)(2,1)}) custom-call(s32[2]{0:T(128)S(1)} %get-tuple-element.136.at_ref, bf16[1024,1536]{1,0:T(8,128)(2,1)} %shard_map.100.refs_0_.refs_1_, bf16[1024,1536]{1,0:T(8,128)(2,1)} %shard_map.100.refs_0_.refs_1_, bf16[256,1536]{1,0:T(8,128)(2,1)S(1)} %collective-permute-done.15.refs_2_, ...), custom_call_target="tpu_custom_call" | custom-call | flops 1 | bytes 1 | tf_op jit(solution)/shard_map/pallas_call | solution.py:207
  169.2 5.5 %collective-permute-start.21 = (bf16[256,1536]{1,0:T(8,128)(2,1)}, bf16[256,1536]{1,0:T(8,128)(2,1)}, u32[]{:S(2)}, u32[]{:S(2)}) collective-permute-start(bf16[256,1536]{1,0:T(8,128)(2,1)} %get-tuple-element.122), channel_id=1, source_target_pairs={{0,2},{1,3},{2,4},{3,5},{4,6},{5,7},{8,10},{9,11},{10,12},{11,13},... | collective-permute-start | bytes 2359304 | tf_op jit(solution)/shard_map/ppermute | solution.py:26
  175.0 1.4 collective-permute-start.22
  176.4 6.1 %shard_map.104 = bf16[256,1024]{1,0:T(8,128)(2,1)} custom-call(bf16[256,3072]{1,0:T(8,128)(2,1)S(1)} %collective-permute-done.14.grads_ref, bf16[1024,3072]{1,0:T(8,128)(2,1)} %shard_map.98.weight_ref), custom_call_target="tpu_custom_call" | custom-call | flops 1 | bytes 1 | tf_op jit(solution)/shard_map/pallas_call | solution.py:235
  183.3 1.5 collective-permute-start.18
  184.8 1.6 copy-done.4
  187.4 2.0 shard_map.105
  189.4 1.5 collective-permute-start.17
  190.9 7.7 %collective-permute-done.22 = bf16[256,1536]{1,0:T(8,128)(2,1)} collective-permute-done((bf16[256,1536]{1,0:T(8,128)(2,1)}, bf16[256,1536]{1,0:T(8,128)(2,1)}, u32[]{:S(2)}, u32[]{:S(2)}) %collective-permute-start.22) | collective-permute-done | bytes 786464 | tf_op jit(solution)/shard_map/ppermute | solution.py:26
  198.6 2.8 %shard_map.108 = bf16[256,2048]{1,0:T(8,128)(2,1)} custom-call(s32[1]{0:T(128)} %bitcast.side_ref, f32[512,1024]{1,0:T(8,128)S(1)} %shard_map.99.mine_ref, bf16[256,1024]{1,0:T(8,128)(2,1)} %collective-permute-done.18.theirs_ref, bf16[512,2048]{1,0:T(8,128)(2,1)S(1)} %bitcast.30, bf16[512,2048]{1,0:T(8,128)(2,1)} %bitcast.40, f32[1,2048]{1,0:T(1,128)S(1)} %copy-done.17), custom_call_target="tpu_custom_call" | custom-call | flops 1 | bytes 1 | tf_op jit(solution)/shard_map/pallas_call | solution.py:274
  202.7 1.9 add_add_fusion.1
  204.7 2.0 add_add_fusion
  206.8 2.0 multiply_reduce_fusion
  209.4 3.0 %collective-permute-done.24 = f32[256]{0:T(256)S(1)} collective-permute-done((f32[256]{0:T(256)S(1)}, f32[256]{0:T(256)S(1)}, u32[]{:S(2)}, u32[]{:S(2)}) %collective-permute-start.24) | collective-permute-done | bytes 1056 | tf_op jit(solution)/shard_map/ppermute | solution.py:325
  212.4 1.5 collective-permute-start.25
  213.9 2.1 collective-permute-done.25
  217.2 3.3 %collective-permute-done.26 = f32[1024]{0:T(1024)S(1)} collective-permute-done((f32[1024]{0:T(1024)S(1)}, f32[1024]{0:T(1024)S(1)}, u32[]{:S(2)}, u32[]{:S(2)}) %collective-permute-start.26) | collective-permute-done | bytes 4128 | tf_op jit(solution)/shard_map/ppermute | solution.py:325
  221.1 2.7 %maximum_bitcast_fusion = bf16[1,512,2048]{2,1,0:T(8,128)(2,1)} fusion(bf16[256,2048]{1,0:T(8,128)(2,1)S(1)} %collective-permute-done.23, bf16[256,2048]{1,0:T(8,128)(2,1)} %collective-permute-done.17), kind=kLoop, calls=%fused_computation.3 | loop fusion | flops 4194304 | bytes 4194304 | tf_op jit(solution)/shard_map/broadcast_in_dim | solution.py:432
  (71 shorter events, 21.4 us)
Async XLA Ops:
  0.6 1.6 copy-start.11
  2.2 0.7 copy-start.16
  2.9 7.6 %copy-start.5 = (bf16[1,256,3072]{2,1,0:T(8,128)(2,1)S(1)}, bf16[1,256,3072]{2,1,0:T(8,128)(2,1)}, u32[]{:S(2)}) copy-start(bf16[1,256,3072]{2,1,0:T(8,128)(2,1)} %param.12) | copy-start | bytes 4718596
  2.9 53.0 %copy-start.18 = (bf16[1,512,3072]{2,1,0:T(8,128)(2,1)S(1)}, bf16[1,512,3072]{2,1,0:T(8,128)(2,1)}, u32[]{:S(2)}) copy-start(bf16[1,512,3072]{2,1,0:T(8,128)(2,1)} %param.11) | copy-start | bytes 9437188
  7.6 49.6 %copy-start.8 = (bf16[1024,512]{1,0:T(8,128)(2,1)}, bf16[1024,512]{1,0:T(8,128)(2,1)S(1)}, u32[]{:S(2)}) copy-start(bf16[1024,512]{1,0:T(8,128)(2,1)S(1)} %get-tuple-element.80.mine_ref) | copy-start | bytes 3145732
  7.6 60.8 %collective-permute-start.4 = (bf16[512,2560]{1,0:T(8,128)(2,1)}, bf16[512,2560]{1,0:T(8,128)(2,1)S(1)}, u32[]{:S(2)}, u32[]{:S(2)}) collective-permute-start(bf16[512,2560]{1,0:T(8,128)(2,1)} %get-tuple-element.74), channel_id=1, source_target_pairs={{0,1},{1,0},{2,3},{3,2},{4,5},{5,4},{6,7},{7,6},{8,9},{9,8},{10,11... | collective-permute-start | bytes 7864328 | tf_op jit(solution)/shard_map/ppermute | solution.py:22
  10.5 36.8 %collective-permute-start = (bf16[256,3072]{1,0:T(8,128)(2,1)S(1)}, bf16[256,3072]{1,0:T(8,128)(2,1)}, u32[]{:S(2)}, u32[]{:S(2)}) collective-permute-start(bf16[256,3072]{1,0:T(8,128)(2,1)S(1)} %bitcast.31), channel_id=1, source_target_pairs={{0,2},{1,3},{2,4},{3,5},{4,6},{5,7},{8,10},{9,11},{10,12},{11,13},... | collective-permute-start | bytes 4718600 | tf_op jit(solution)/shard_map/ppermute | solution.py:26
  15.1 37.6 %collective-permute-start.1 = (bf16[256,3072]{1,0:T(8,128)(2,1)S(1)}, bf16[256,3072]{1,0:T(8,128)(2,1)}, u32[]{:S(2)}, u32[]{:S(2)}) collective-permute-start(bf16[256,3072]{1,0:T(8,128)(2,1)S(1)} %bitcast.32), channel_id=1, source_target_pairs={{2,0},{3,1},{4,2},{5,3},{6,4},{7,5},{10,8},{11,9},{12,10},{13,11},... | collective-permute-start | bytes 4718600 | tf_op jit(solution)/shard_map/ppermute | solution.py:26
  52.7 31.6 %collective-permute-start.2 = (bf16[256,3072]{1,0:T(8,128)(2,1)}, bf16[256,3072]{1,0:T(8,128)(2,1)}, u32[]{:S(2)}, u32[]{:S(2)}) collective-permute-start(bf16[256,3072]{1,0:T(8,128)(2,1)} %collective-permute-done.refs_0_), channel_id=1, source_target_pairs={{2,4},{3,5},{4,6},{5,7},{10,12},{11,13},{12,14},{13,15},{18,20},{1... | collective-permute-start | bytes 4718600 | tf_op jit(solution)/shard_map/ppermute | solution.py:26
  54.6 38.1 %collective-permute-start.3 = (bf16[256,3072]{1,0:T(8,128)(2,1)}, bf16[256,3072]{1,0:T(8,128)(2,1)}, u32[]{:S(2)}, u32[]{:S(2)}) collective-permute-start(bf16[256,3072]{1,0:T(8,128)(2,1)} %collective-permute-done.1.refs_3_), channel_id=1, source_target_pairs={{2,0},{3,1},{4,2},{5,3},{10,8},{11,9},{12,10},{13,11},{18,16},{19,... | collective-permute-start | bytes 4718600 | tf_op jit(solution)/shard_map/ppermute | solution.py:26
  57.2 46.5 %collective-permute-start.10 = (bf16[512,1536]{1,0:T(8,128)(2,1)}, bf16[512,1536]{1,0:T(8,128)(2,1)}, u32[]{:S(2)}, u32[]{:S(2)}) collective-permute-start(bf16[512,1536]{1,0:T(8,128)(2,1)} %slice.17), channel_id=1, source_target_pairs={{0,1},{1,0},{2,3},{3,2},{4,5},{5,4},{6,7},{7,6},{8,9},{9,8},{10,11... | collective-permute-start | bytes 4718600 | tf_op jit(solution)/shard_map/ppermute | solution.py:22
  68.4 1.2 copy-start.9
  76.0 1.9 copy-start
  77.9 4.5 %copy-start.3 = (bf16[1,512,3072]{2,1,0:T(8,128)(2,1)S(1)}, bf16[1,512,3072]{2,1,0:T(8,128)(2,1)}, u32[]{:S(2)}) copy-start(bf16[1,512,3072]{2,1,0:T(8,128)(2,1)} %param.9) | copy-start | bytes 9437188
  78.1 19.1 %collective-permute-start.7 = (bf16[256,1536]{1,0:T(8,128)(2,1)S(1)}, bf16[256,1536]{1,0:T(8,128)(2,1)S(1)}, u32[]{:S(2)}, u32[]{:S(2)}) collective-permute-start(bf16[256,1536]{1,0:T(8,128)(2,1)S(1)} %shard_map.96), channel_id=1, source_target_pairs={{0,2},{1,3},{6,4},{7,5},{8,10},{9,11},{14,12},{15,13},{16,18},{17,... | collective-permute-start | bytes 2359304 | tf_op jit(solution)/shard_map/ppermute | solution.py:80
  92.7 31.1 %collective-permute-start.5 = (bf16[256,3072]{1,0:T(8,128)(2,1)}, bf16[256,3072]{1,0:T(8,128)(2,1)}, u32[]{:S(2)}, u32[]{:S(2)}) collective-permute-start(bf16[256,3072]{1,0:T(8,128)(2,1)} %collective-permute-done.2.refs_1_), channel_id=1, source_target_pairs={{4,6},{5,7},{12,14},{13,15},{20,22},{21,23},{28,30},{29,31}} | collective-permute-start | bytes 4718600 | tf_op jit(solution)/shard_map/ppermute | solution.py:26
  94.5 35.9 %collective-permute-start.6 = (bf16[256,3072]{1,0:T(8,128)(2,1)}, bf16[256,3072]{1,0:T(8,128)(2,1)}, u32[]{:S(2)}, u32[]{:S(2)}) collective-permute-start(bf16[256,3072]{1,0:T(8,128)(2,1)} %collective-permute-done.3.refs_4_), channel_id=1, source_target_pairs={{2,0},{3,1},{10,8},{11,9},{18,16},{19,17},{26,24},{27,25}} | collective-permute-start | bytes 4718600 | tf_op jit(solution)/shard_map/ppermute | solution.py:26
  97.2 8.0 %copy-start.10 = (bf16[1024,512]{1,0:T(8,128)(2,1)S(1)}, bf16[1024,512]{1,0:T(8,128)(2,1)}, u32[]{:S(2)}) copy-start(bf16[1024,512]{1,0:T(8,128)(2,1)} %copy-done.8) | copy-start | bytes 3145732
  98.5 18.5 %collective-permute-start.8 = (bf16[256,1536]{1,0:T(8,128)(2,1)S(1)}, bf16[256,1536]{1,0:T(8,128)(2,1)S(1)}, u32[]{:S(2)}, u32[]{:S(2)}) collective-permute-start(bf16[256,1536]{1,0:T(8,128)(2,1)S(1)} %get-tuple-element.84), channel_id=1, source_target_pairs={{0,2},{1,3},{2,4},{3,5},{8,10},{9,11},{10,12},{11,13},{16,18},{17,... | collective-permute-start | bytes 2359304 | tf_op jit(solution)/shard_map/ppermute | solution.py:26
  103.0 18.5 %collective-permute-start.9 = (bf16[256,1536]{1,0:T(8,128)(2,1)S(1)}, bf16[256,1536]{1,0:T(8,128)(2,1)S(1)}, u32[]{:S(2)}, u32[]{:S(2)}) collective-permute-start(bf16[256,1536]{1,0:T(8,128)(2,1)S(1)} %get-tuple-element.85), channel_id=1, source_target_pairs={{4,2},{5,3},{6,4},{7,5},{12,10},{13,11},{14,12},{15,13},{20,18},{2... | collective-permute-start | bytes 2359304 | tf_op jit(solution)/shard_map/ppermute | solution.py:26
  103.7 38.2 %collective-permute-start.11 = (bf16[256,3072]{1,0:T(8,128)(2,1)}, bf16[256,3072]{1,0:T(8,128)(2,1)}, u32[]{:S(2)}, u32[]{:S(2)}) collective-permute-start(bf16[256,3072]{1,0:T(8,128)(2,1)} %get-tuple-element.95), channel_id=1, source_target_pairs={{0,1},{1,0},{2,3},{3,2},{4,5},{5,4},{6,7},{7,6},{8,9},{9,8},{10,11... | collective-permute-start | bytes 4718600 | tf_op jit(solution)/shard_map/ppermute | solution.py:22
  111.8 1.9 copy-start.1
  113.7 16.7 %copy-start.6 = (bf16[1,256,3072]{2,1,0:T(8,128)(2,1)S(1)}, bf16[1,256,3072]{2,1,0:T(8,128)(2,1)}, u32[]{:S(2)}) copy-start(bf16[1,256,3072]{2,1,0:T(8,128)(2,1)} %param.12) | copy-start | bytes 4718596
  117.0 18.1 %collective-permute-start.12 = (bf16[256,1536]{1,0:T(8,128)(2,1)S(1)}, bf16[256,1536]{1,0:T(8,128)(2,1)S(1)}, u32[]{:S(2)}, u32[]{:S(2)}) collective-permute-start(bf16[256,1536]{1,0:T(8,128)(2,1)S(1)} %shard_map.101), channel_id=1, source_target_pairs={{0,2},{1,3},{6,4},{7,5},{8,10},{9,11},{14,12},{15,13},{16,18},{17,... | collective-permute-start | bytes 2359304 | tf_op jit(solution)/shard_map/ppermute | solution.py:80
  121.4 0.9 copy-start.12
  122.3 52.7 %collective-permute-start.14 = (bf16[256,3072]{1,0:T(8,128)(2,1)}, bf16[256,3072]{1,0:T(8,128)(2,1)S(1)}, u32[]{:S(2)}, u32[]{:S(2)}) collective-permute-start(bf16[256,3072]{1,0:T(8,128)(2,1)} %get-tuple-element.104), channel_id=1, source_target_pairs={{0,1},{1,0},{2,3},{3,2},{4,5},{5,4},{6,7},{7,6},{8,9},{9,8},{10,11... | collective-permute-start | bytes 4718600 | tf_op jit(solution)/shard_map/ppermute | solution.py:22
  130.4 5.6 %copy-start.2 = (bf16[1024,1536]{1,0:T(8,128)(2,1)S(1)}, bf16[1024,1536]{1,0:T(8,128)(2,1)}, u32[]{:S(2)}) copy-start(bf16[1024,1536]{1,0:T(8,128)(2,1)} %shard_map.100.refs_0_.refs_1_) | copy-start | bytes 9437188
  138.0 27.0 %collective-permute-start.15 = (bf16[256,1536]{1,0:T(8,128)(2,1)}, bf16[256,1536]{1,0:T(8,128)(2,1)S(1)}, u32[]{:S(2)}, u32[]{:S(2)}) collective-permute-start(bf16[256,1536]{1,0:T(8,128)(2,1)} %get-tuple-element.106), channel_id=1, source_target_pairs={{0,2},{1,3},{2,4},{3,5},{8,10},{9,11},{10,12},{11,13},{16,18},{17,... | collective-permute-start | bytes 2359304 | tf_op jit(solution)/shard_map/ppermute | solution.py:26
  141.0 8.3 %copy-start.13 = (bf16[256,1536]{1,0:T(8,128)(2,1)S(1)}, bf16[256,1536]{1,0:T(8,128)(2,1)}, u32[]{:S(2)}) copy-start(bf16[256,1536]{1,0:T(8,128)(2,1)} %copy-done.12) | copy-start | bytes 2359300
  141.0 25.2 %collective-permute-start.16 = (bf16[256,1536]{1,0:T(8,128)(2,1)S(1)}, bf16[256,1536]{1,0:T(8,128)(2,1)S(1)}, u32[]{:S(2)}, u32[]{:S(2)}) collective-permute-start(bf16[256,1536]{1,0:T(8,128)(2,1)S(1)} %get-tuple-element.107), channel_id=1, source_target_pairs={{4,2},{5,3},{6,4},{7,5},{12,10},{13,11},{14,12},{15,13},{20,18},{2... | collective-permute-start | bytes 2359304 | tf_op jit(solution)/shard_map/ppermute | solution.py:26
  147.8 34.7 %collective-permute-start.13 = (bf16[256,1024]{1,0:T(8,128)(2,1)S(1)}, bf16[256,1024]{1,0:T(8,128)(2,1)S(1)}, u32[]{:S(2)}, u32[]{:S(2)}) collective-permute-start(bf16[256,1024]{1,0:T(8,128)(2,1)S(1)} %shard_map.102), channel_id=1, source_target_pairs={{0,1},{1,0},{2,3},{3,2},{4,5},{5,4},{6,7},{7,6},{8,9},{9,8},{10,11... | collective-permute-start | bytes 1572872 | tf_op jit(solution)/shard_map/ppermute | solution.py:22
  152.3 37.1 %collective-permute-start.19 = (bf16[256,1536]{1,0:T(8,128)(2,1)}, bf16[256,1536]{1,0:T(8,128)(2,1)}, u32[]{:S(2)}, u32[]{:S(2)}) collective-permute-start(bf16[256,1536]{1,0:T(8,128)(2,1)} %get-tuple-element.118), channel_id=1, source_target_pairs={{0,2},{1,3},{2,4},{3,5},{4,6},{5,7},{8,10},{9,11},{10,12},{11,13},... | collective-permute-start | bytes 2359304 | tf_op jit(solution)/shard_map/ppermute | solution.py:26
  165.0 25.9 %collective-permute-start.20 = (bf16[256,1536]{1,0:T(8,128)(2,1)}, bf16[256,1536]{1,0:T(8,128)(2,1)}, u32[]{:S(2)}, u32[]{:S(2)}) collective-permute-start(bf16[256,1536]{1,0:T(8,128)(2,1)} %get-tuple-element.119), channel_id=1, source_target_pairs={{2,0},{3,1},{4,2},{5,3},{6,4},{7,5},{10,8},{11,9},{12,10},{13,11},... | collective-permute-start | bytes 2359304 | tf_op jit(solution)/shard_map/ppermute | solution.py:26
  169.2 21.7 %collective-permute-start.21 = (bf16[256,1536]{1,0:T(8,128)(2,1)}, bf16[256,1536]{1,0:T(8,128)(2,1)}, u32[]{:S(2)}, u32[]{:S(2)}) collective-permute-start(bf16[256,1536]{1,0:T(8,128)(2,1)} %get-tuple-element.122), channel_id=1, source_target_pairs={{0,2},{1,3},{2,4},{3,5},{4,6},{5,7},{8,10},{9,11},{10,12},{11,13},... | collective-permute-start | bytes 2359304 | tf_op jit(solution)/shard_map/ppermute | solution.py:26
  175.0 9.8 %copy-start.17 = (f32[1,2048]{1,0:T(1,128)S(1)}, f32[1,2048]{1,0:T(1,128)}, u32[]{:S(2)}) copy-start(f32[1,2048]{1,0:T(1,128)} %gain_ref.1) | copy-start | bytes 24580
  175.0 23.6 %collective-permute-start.22 = (bf16[256,1536]{1,0:T(8,128)(2,1)}, bf16[256,1536]{1,0:T(8,128)(2,1)}, u32[]{:S(2)}, u32[]{:S(2)}) collective-permute-start(bf16[256,1536]{1,0:T(8,128)(2,1)} %get-tuple-element.123), channel_id=1, source_target_pairs={{2,0},{3,1},{4,2},{5,3},{6,4},{7,5},{10,8},{11,9},{12,10},{13,11},... | collective-permute-start | bytes 2359304 | tf_op jit(solution)/shard_map/ppermute | solution.py:26
  182.5 0.8 copy-start.14
  183.3 15.3 %collective-permute-start.18 = (bf16[256,1024]{1,0:T(8,128)(2,1)}, bf16[256,1024]{1,0:T(8,128)(2,1)}, u32[]{:S(2)}, u32[]{:S(2)}) collective-permute-start(bf16[256,1024]{1,0:T(8,128)(2,1)} %shard_map.104), channel_id=1, source_target_pairs={{0,1},{1,0},{2,3},{3,2},{4,5},{5,4},{6,7},{7,6},{8,9},{9,8},{10,11... | collective-permute-start | bytes 1572872 | tf_op jit(solution)/shard_map/ppermute | solution.py:22
  184.8 1.6 copy-start.4
  186.4 1.0 copy-start.15
  189.4 31.7 %collective-permute-start.17 = (bf16[256,2048]{1,0:T(8,128)(2,1)S(1)}, bf16[256,2048]{1,0:T(8,128)(2,1)}, u32[]{:S(2)}, u32[]{:S(2)}) collective-permute-start(bf16[256,2048]{1,0:T(8,128)(2,1)S(1)} %shard_map.105), channel_id=1, source_target_pairs={{8,0},{16,8},{24,16},{9,1},{17,9},{25,17},{10,2},{18,10},{26,18},{... | collective-permute-start | bytes 3145736 | tf_op jit(solution)/shard_map/ppermute | solution.py:379
  201.5 19.6 %collective-permute-start.23 = (bf16[256,2048]{1,0:T(8,128)(2,1)}, bf16[256,2048]{1,0:T(8,128)(2,1)S(1)}, u32[]{:S(2)}, u32[]{:S(2)}) collective-permute-start(bf16[256,2048]{1,0:T(8,128)(2,1)} %shard_map.108), channel_id=1, source_target_pairs={{8,0},{16,8},{24,16},{9,1},{17,9},{25,17},{10,2},{18,10},{26,18},{... | collective-permute-start | bytes 3145736 | tf_op jit(solution)/shard_map/ppermute | solution.py:379
  204.6 2.1 copy-start.7
  208.8 3.6 %collective-permute-start.24 = (f32[256]{0:T(256)S(1)}, f32[256]{0:T(256)S(1)}, u32[]{:S(2)}, u32[]{:S(2)}) collective-permute-start(f32[256]{0:T(256)S(1)} %div.26), channel_id=1, source_target_pairs={{0,1},{1,0},{2,3},{3,2},{4,5},{5,4},{6,7},{7,6},{8,9},{9,8},{10,11... | collective-permute-start | bytes 3080 | tf_op jit(solution)/shard_map/ppermute | solution.py:325
  212.4 3.6 %collective-permute-start.25 = (f32[512]{0:T(512)S(1)}, f32[512]{0:T(512)S(1)}, u32[]{:S(2)}, u32[]{:S(2)}) collective-permute-start(f32[512]{0:T(512)S(1)} %maximum_select_fusion.1), channel_id=1, source_target_pairs={{0,2},{1,3},{2,0},{3,1},{4,6},{5,7},{6,4},{7,5},{8,10},{9,11},{10,... | collective-permute-start | bytes 6152 | tf_op jit(solution)/shard_map/ppermute | solution.py:325
  216.0 4.5 %collective-permute-start.26 = (f32[1024]{0:T(1024)S(1)}, f32[1024]{0:T(1024)S(1)}, u32[]{:S(2)}, u32[]{:S(2)}) collective-permute-start(f32[1024]{0:T(1024)S(1)} %maximum_select_fusion), channel_id=1, source_target_pairs={{0,4},{1,5},{2,6},{3,7},{4,0},{5,1},{6,2},{7,3},{8,12},{9,13},{10,... | collective-permute-start | bytes 12296 | tf_op jit(solution)/shard_map/ppermute | solution.py:325

commit v2 on v1

v2 whole, which is shorter than its diff:
```python
import math

import jax
import jax.numpy as jnp
from jax import lax
from jax.experimental import pallas as pl
from jax.experimental.pallas import tpu as pltpu
from jax.sharding import PartitionSpec as P

EPS = 1e-05
BF16 = jnp.bfloat16
F32 = jnp.float32


def row_scale(rows):
    values = rows.astype(F32)
    return lax.rsqrt(jnp.mean(values * values, axis=-1, keepdims=True) + EPS)


def swap(value, axis):
    count = lax.axis_size(axis)
    return lax.ppermute(value, axis, [(i, i ^ 1) for i in range(count)])


def hop(value, axis, sources, step):
    return lax.ppermute(
        value, axis, [(2 * o + q, 2 * (o + step) + q) for o in sources for q in range(2)]
    )


def split_halves(array, owned):
    pieces = [array[..., i : i + owned] for i in range(0, array.shape[-1], owned)]
    return jnp.concatenate(pieces[0::2], axis=-1), jnp.concatenate(pieces[1::2], axis=-1)


def join_halves(even, odd, owned):
    pieces = []
    for i in range(0, even.shape[-1], owned):
        pieces += [even[..., i : i + owned], odd[..., i : i + owned]]
    return jnp.concatenate(pieces, axis=-1)


class Gather:
    def __init__(self, shard, axis, pairs, pair):
        self.shard, self.axis, self.pairs, self.pair = shard, axis, pairs, pair
        self.ups, self.downs, self.flying = [], [], []
        self.advance()

    def advance(self):
        if self.flying:
            self.ups.append(self.flying[0])
            self.downs.append(self.flying[1])
        r = len(self.ups) + 1
        up = hop(([self.shard] + self.ups)[-1], self.axis, range(r - 1, self.pairs - 1), 1)
        down = hop(([self.shard] + self.downs)[-1], self.axis, range(1, self.pairs - r + 1), -1)
        self.flying = [up, down]

    def done(self):
        return len(self.ups) == self.pairs - 2

    def whole(self):
        return assemble(self.pair, self.shard, self.ups + self.flying[:1], self.downs + self.flying[1:])


class Scatter:
    def __init__(self, term, axis, pairs, pair, owned, line):
        self.term, self.axis, self.pairs, self.pair, self.owned = term, axis, pairs, pair, owned
        self.line = line
        self.step, self.flying = 0, []
        self.advance()

    def advance(self):
        self.step += 1
        s, pairs, pair = self.step, self.pairs, self.pair
        above = jnp.minimum(pair + pairs - s, pairs - 1)
        below = jnp.maximum(pair - pairs + s, 0)
        if s == 1 and pairs >= 4:
            (send,) = pick_and_add(self.term, [jnp.where(pair < pairs // 2, above, below)], [], self.owned)
            route = [(q, 2 + q) for q in range(2)]
            route += [(2 * pairs - 2 + q, 2 * pairs - 4 + q) for q in range(2)]
            self.flying = [lax.ppermute(send, self.axis, route)]
            return
        came = [self.flying[0], self.flying[-1]] if self.flying else []
        send_up, send_down = self.line.arrived(*pick_and_add(self.term, [above, below], came, self.owned))
        self.flying = [
            hop(send_up, self.axis, range(s), 1),
            hop(send_down, self.axis, range(pairs - s, pairs), -1),
        ]

    def done(self):
        return self.step == self.pairs - 1


SMALL = pl.CostEstimate(flops=1, bytes_accessed=1, transcendentals=0)
VMEM = pl.BlockSpec(memory_space=pltpu.VMEM)
SMEM = pl.BlockSpec(memory_space=pltpu.SMEM)
ANY = pl.BlockSpec(memory_space=pl.ANY)
WHOLE = pltpu.CompilerParams(vmem_limit_bytes=60 * 1024 * 1024)
PARAMS = pltpu.CompilerParams(vmem_limit_bytes=24 * 1024 * 1024)


def assemble(pair, shard, ups, downs):
    pairs, owned = len(ups) + 1, shard.shape[0]

    def kernel(pair_ref, shard_ref, *refs):
        up_refs, down_refs = refs[: pairs - 1], refs[pairs - 1 : 2 * pairs - 2]
        out_ref, slots, came, gone = refs[2 * pairs - 2 :]
        here = pair_ref[0]

        def bring(source, at):
            return pltpu.make_async_copy(source, slots.at[at], came.at[at])

        def put(at):
            return pltpu.make_async_copy(slots.at[at], out_ref.at[pl.ds(at * owned, owned)], gone.at[at])

        for at in range(pairs):
            for source_pair in range(pairs):
                distance = source_pair - at
                if distance == 0:
                    source = shard_ref
                elif distance > 0:
                    source = up_refs[distance - 1]
                else:
                    source = down_refs[-distance - 1]

                @pl.when(here == source_pair)
                def _(source=source, at=at):
                    bring(source, at).start()

        for at in range(pairs):
            bring(shard_ref, at).wait()
            put(at).start()
        for at in range(pairs):
            put(at).wait()

    return pl.pallas_call(
        kernel,
        out_shape=jax.ShapeDtypeStruct((pairs * owned, shard.shape[1]), shard.dtype),
        in_specs=[pl.BlockSpec(memory_space=pltpu.SMEM)] + [pl.BlockSpec(memory_space=pl.ANY)] * (2 * pairs - 1),
        out_specs=pl.BlockSpec(memory_space=pl.ANY),
        scratch_shapes=[
            pltpu.VMEM((pairs,) + shard.shape, shard.dtype),
            pltpu.SemaphoreType.DMA((pairs,)),
            pltpu.SemaphoreType.DMA((pairs,)),
        ],
        compiler_params=PARAMS,
        cost_estimate=SMALL,
    )(pair.reshape(1), shard, *ups, *downs)


def first_packet(rows, gain, grads, wide, side, owned):
    tokens, features = rows.shape
    half = features // 2
    blocks = 4
    block = tokens // blocks

    def kernel(side_ref, gain_ref, rows_any, grads_any, mine_ref, packet_ref, rows_ref, sems):
        def bring(i):
            here = pl.ds(i * block, block)
            return pltpu.make_async_copy(rows_any.at[here], rows_ref.at[here], sems.at[i])

        beside = pltpu.make_async_copy(grads_any.at[:, :wide], packet_ref.at[:, half:], sems.at[blocks])
        for i in range(blocks):
            bring(i).start()
        beside.start()
        first = side_ref[0] == 0
        for i in range(blocks):
            bring(i).wait()
            here = slice(i * block, (i + 1) * block)
            values = rows_ref[here, :].astype(F32)
            scale = lax.rsqrt(jnp.mean(values * values, axis=-1, keepdims=True) + EPS)
            normed = (values * scale * gain_ref[...]).astype(BF16)
            even, odd = split_halves(normed, owned)
            mine_ref[:, here] = jnp.where(first, even, odd).T
            packet_ref[here, :half] = jnp.where(first, odd, even)
        beside.wait()

    return pl.pallas_call(
        kernel,
        in_specs=[SMEM, VMEM, ANY, ANY],
        out_specs=[VMEM, VMEM],
        out_shape=[
            jax.ShapeDtypeStruct((half, tokens), BF16),
            jax.ShapeDtypeStruct((tokens, half + wide), BF16),
        ],
        scratch_shapes=[pltpu.VMEM((tokens, features), BF16), pltpu.SemaphoreType.DMA((blocks + 1,))],
        compiler_params=WHOLE,
        cost_estimate=SMALL,
    )(side.reshape(1), gain[None, :], rows, grads)


def pick_and_add(term, places, came, owned):
    wide = term.shape[1]
    count = len(places)

    def kernel(at_ref, term_any, *refs):
        came_refs, out_refs = refs[: len(came)], refs[len(came) : len(came) + count]
        picked, sems = refs[len(came) + count :]
        copies = []
        for i in range(count):
            start = pl.multiple_of(at_ref[i] * owned, owned)
            target = picked.at[i] if came else out_refs[i]
            copies.append(pltpu.make_async_copy(term_any.at[pl.ds(start, owned)], target, sems.at[i]))
        for copy in copies:
            copy.start()
        for i, copy in enumerate(copies):
            copy.wait()
            if came:
                out_refs[i][...] = (picked[i].astype(F32) + came_refs[i][...].astype(F32)).astype(BF16)

    return pl.pallas_call(
        kernel,
        in_specs=[SMEM, ANY] + [VMEM] * len(came),
        out_specs=[VMEM] * count,
        out_shape=[jax.ShapeDtypeStruct((owned, wide), BF16)] * count,
        scratch_shapes=[pltpu.VMEM((count, owned, wide), BF16), pltpu.SemaphoreType.DMA((count,))],
        compiler_params=PARAMS,
        cost_estimate=SMALL,
    )(jnp.stack(places), term, *came)


def transpose_product(pieces, weight, dtype):
    features = weight.shape[0]
    rows = [piece.shape[0] for piece in pieces]
    block = min(256, features)

    def kernel(*refs):
        weight_ref, out_ref = refs[-2:]
        for i, piece_ref in enumerate(refs[:-2]):
            top = sum(rows[:i])
            for at in range(0, features, block):
                out_ref[top : top + rows[i], at : at + block] = lax.dot_general(
                    piece_ref[...], weight_ref[at : at + block, :], (((1,), (1,)), ((), ())),
                    preferred_element_type=F32,
                ).astype(dtype)

    return pl.pallas_call(
        kernel,
        in_specs=[VMEM] * (len(pieces) + 1),
        out_specs=VMEM,
        out_shape=jax.ShapeDtypeStruct((sum(rows), features), dtype),
        compiler_params=PARAMS,
        cost_estimate=SMALL,
    )(*pieces, weight)


def input_gradient(mine, theirs, start, rows, resid, gain, side, owned, cost):
    tokens, half = theirs.shape
    block = min(64, tokens)

    def kernel(side_ref, mine_ref, theirs_ref, rows_ref, resid_ref, gain_ref, out_ref):
        first = side_ref[0] == 0

        def part(i, carry):
            here = pl.ds(pl.multiple_of(i * block, block), block)
            mine_part = mine_ref[pl.ds(pl.multiple_of(start + i * block, block), block), :]
            theirs_part = theirs_ref[here, :].astype(F32)
            even = jnp.where(first, mine_part, theirs_part)
            odd = jnp.where(first, theirs_part, mine_part)
            values = rows_ref[here, :].astype(F32)
            scale = lax.rsqrt(jnp.mean(values * values, axis=-1, keepdims=True) + EPS)
            gained = gain_ref[...] * join_halves(even, odd, owned)
            inner = jnp.mean(gained * values, axis=-1, keepdims=True)
            out_ref[here, :] = (
                resid_ref[here, :].astype(F32) + scale * gained - values * (scale * scale * scale * inner)
            ).astype(BF16)
            return carry

        lax.fori_loop(0, tokens // block, part, 0)

    return pl.pallas_call(
        kernel,
        in_specs=[SMEM] + [VMEM] * 5,
        out_specs=VMEM,
        out_shape=jax.ShapeDtypeStruct((tokens, 2 * half), BF16),
        compiler_params=PARAMS,
        cost_estimate=cost,
    )(side.reshape(1), mine, theirs, rows, resid, gain[None, :])


def owned_sums(chains, weight_rows, pair, owned):
    each = [[chain.term, *chain.flying] for chain in chains]
    came = [array for arrays in each for array in arrays[1:]]
    wides = [arrays[0].shape[1] for arrays in each]

    def kernel(pair_ref, weight_any, *refs):
        terms, came_refs = refs[: len(each)], refs[len(each) : len(each) + len(came)]
        total_ref, part_ref = refs[len(each) + len(came) :][:2]
        own_refs, (weight_ref, sems) = refs[len(each) + len(came) + 2 : -2], refs[-2:]
        start = pl.multiple_of(pair_ref[0] * owned, owned)
        copies = [
            pltpu.make_async_copy(terms[i].at[pl.ds(start, owned)], own_refs[i], sems.at[i]) for i in range(len(each))
        ]
        copies.append(pltpu.make_async_copy(weight_any, weight_ref, sems.at[len(each)]))
        for copy in copies:
            copy.start()
        for copy in copies:
            copy.wait()
        along = jnp.zeros((owned, 128), F32)
        column = at = 0
        for i, arrays in enumerate(each):
            for left in range(0, wides[i], 128):
                here = slice(left, left + 128)
                total = own_refs[i][:, here].astype(F32)
                for k in range(len(arrays) - 1):
                    total = total + came_refs[at + k][:, here].astype(F32)
                total_ref[:, column : column + 128] = total
                along = along + weight_ref[:, column : column + 128].astype(F32) * total
                column += 128
            at += len(arrays) - 1
        part_ref[...] = jnp.sum(along.T, axis=0, keepdims=True)

    return pl.pallas_call(
        kernel,
        in_specs=[SMEM, ANY] + [ANY] * len(each) + [VMEM] * len(came),
        out_specs=[VMEM, VMEM],
        out_shape=[jax.ShapeDtypeStruct((owned, sum(wides)), F32), jax.ShapeDtypeStruct((1, owned), F32)],
        scratch_shapes=[pltpu.VMEM((owned, wide), BF16) for wide in wides]
        + [pltpu.VMEM(weight_rows.shape, BF16), pltpu.SemaphoreType.DMA((len(each) + 1,))],
        compiler_params=PARAMS,
        cost_estimate=SMALL,
    )(pair.reshape(1), weight_rows, *[arrays[0] for arrays in each], *came)


def weight_term(mine, theirs, grads, start, got, got_start):
    features, tokens = mine.shape
    wide = got.shape[1] - got_start
    block = math.gcd(512, wide)
    fresh = theirs is None

    def kernel(mine_any, grads_any, got_any, *refs):
        theirs_any = got_any.at[:, :features] if fresh else refs[0]
        out_ref, mine_ref, grads_ref, got_ref, theirs_ref, sems = refs[-6:]
        copies = [
            pltpu.make_async_copy(theirs_any, theirs_ref, sems.at[0]),
            pltpu.make_async_copy(mine_any, mine_ref, sems.at[1]),
            pltpu.make_async_copy(grads_any.at[:, start : start + wide], grads_ref, sems.at[2]),
            pltpu.make_async_copy(got_any.at[:, got_start : got_start + wide], got_ref, sems.at[3]),
        ]
        for copy in copies:
            copy.start()
        copies[0].wait()
        if fresh:
            flipped = refs[0]
            flipped[...] = theirs_ref[...].T
        else:
            flipped = theirs_ref
        for copy in copies[1:]:
            copy.wait()
        for at in range(0, wide, block):
            total = jnp.dot(mine_ref[...], grads_ref[:, at : at + block], preferred_element_type=F32)
            total += jnp.dot(flipped[...], got_ref[:, at : at + block], preferred_element_type=F32)
            out_ref[:, at : at + block] = total.astype(BF16)

    out_shape = [jax.ShapeDtypeStruct((features, wide), BF16)]
    if fresh:
        out_shape.insert(0, jax.ShapeDtypeStruct((features, tokens), BF16))
    operands = [mine, grads, got] + ([] if fresh else [theirs])
    outs = pl.pallas_call(
        kernel,
        in_specs=[ANY] * len(operands),
        out_specs=[VMEM] * len(out_shape),
        out_shape=out_shape,
        scratch_shapes=[
            pltpu.VMEM((features, tokens), BF16),
            pltpu.VMEM((tokens, wide), BF16),
            pltpu.VMEM((tokens, wide), BF16),
            pltpu.VMEM((tokens, features) if fresh else (features, tokens), BF16),
            pltpu.SemaphoreType.DMA((4,)),
        ],
        compiler_params=PARAMS,
        cost_estimate=SMALL,
    )(*operands)
    return outs if fresh else (theirs, outs[0])


class Line:
    def __init__(self, token):
        self.token = token

    def arrived(self, *values):
        *values, self.token = lax.optimization_barrier((*values, self.token))
        return values if len(values) > 1 else values[0]

    def meet(self, chains, *values):
        flat = [array for chain in chains for array in chain.flying]
        flat = lax.optimization_barrier((*flat, *values, self.token))
        at = 0
        for chain in chains:
            chain.flying = list(flat[at : at + len(chain.flying)])
            at += len(chain.flying)
        self.token = flat[-1]
        return flat[at:-1]


def local(layer_input, resid_grad, qkv_grad, prev_input, prev_qkv_grad, qkv_weight, norm_gain):
    axis = "fsdp"
    rows_now, resid, grads_now = layer_input[0], resid_grad[0], qkv_grad[0]
    rows_prev, grads_prev = prev_input[0], prev_qkv_grad[0]
    weight_rows, gain = qkv_weight[0], norm_gain[0]
    owned, columns = weight_rows.shape
    tokens = rows_now.shape[0]
    count = lax.axis_size(axis)
    pairs = count // 2
    me = lax.axis_index(axis)
    pair, side = me // 2, lax.rem(me, 2)
    first = side == 0
    layers = lax.axis_size("section")
    line = Line(gain)

    cuts = [0, columns * 5 // 12, columns]
    bounds = [0, tokens // 2, tokens]

    def summing(term):
        return Scatter(term, axis, pairs, pair, owned, line)

    helped, stands_in = 2, lax.axis_index("section") == 0
    layer_list = list(range(layers))

    def to_stand_in(own):
        return lax.ppermute(own, "section", [(helped, 0)])

    def swap_in_layers(value, idle):
        return lax.ppermute(
            value,
            ("section", axis),
            [(k * count + i, k * count + (i ^ 1)) for k in layer_list if k != idle for i in range(count)],
        )

    def back(piece, idle):
        return swap_in_layers(line.arrived(transpose_product([piece], weight_half, BF16)), idle)

    def up_a_layer(i, theirs, cost=SMALL):
        rows, resid, gain_of = part_inputs[i]
        local_grad = line.arrived(
            input_gradient(direction_mine, theirs, bounds[i], rows, resid, gain_of, side, owned, cost)
        )
        route = [(k, k - 1) for k in layer_list[1:]]
        if i == 1:
            route = [(0 if k == helped else k, k - 1) for k in layer_list[1:]]
        return lax.ppermute(local_grad, "section", route)

    normed_mine, packet = first_packet(rows_prev, gain, grads_prev, cuts[1], side, owned)
    packet = swap(line.arrived(packet), axis)
    weight_there, gain_there = line.arrived(to_stand_in(weight_rows), to_stand_in(gain))
    gather = Gather(jnp.where(stands_in, weight_there, weight_rows), axis, pairs, pair)
    gain_second = jnp.where(stands_in, gain_there, gain)
    seconds = [grads_now[bounds[1] :], rows_now[bounds[1] :], resid[bounds[1] :]]
    there = to_stand_in(jnp.concatenate(seconds, axis=1))
    x2 = swap(line.arrived(grads_prev)[:, cuts[1] :], axis)

    line.meet([gather])
    gather.advance()
    (packet,) = line.meet([], packet)
    normed_theirs, term0 = weight_term(normed_mine, None, grads_prev, cuts[0], packet, normed_mine.shape[0])
    sum0 = summing(term0)
    now_first = line.arrived(grads_now[: bounds[1]])
    g0 = swap_in_layers(now_first, 0)
    line.meet([gather])
    gather.advance()
    line.meet([sum0])
    sum0.advance()
    x2, there = line.meet([], x2, there)
    edges = [0, columns, columns + rows_now.shape[1], there.shape[1]]
    now_second, rows_second, resid_second = [
        jnp.where(stands_in, there[:, edges[i] : edges[i + 1]], seconds[i]) for i in range(3)
    ]
    g1 = swap_in_layers(line.arrived(now_second), helped)
    unused, term1 = weight_term(normed_mine, normed_theirs, grads_prev, cuts[1], x2, 0)
    sum1 = summing(term1)
    line.meet([sum0])
    sum0.advance()
    line.meet([gather])
    while not gather.done():
        gather.advance()
        line.meet([gather])
    weight_half = gather.whole()
    direction_mine = line.arrived(transpose_product([now_first, now_second], weight_half, F32))
    part_inputs = [(rows_now[: bounds[1]], resid[: bounds[1]], gain), (rows_second, resid_second, gain_second)]
    line.meet([sum1])
    sum1.advance()
    (g0,) = line.meet([], g0)
    r0 = back(g0, 0)
    line.meet([sum1])
    sum1.advance()
    (g1,) = line.meet([], g1)
    r1 = back(g1, helped)
    line.meet([sum0])
    r0 = line.arrived(r0)
    u0 = up_a_layer(0, r0)
    r1 = line.arrived(r1)
    u1 = up_a_layer(1, r1)
    line.meet([sum0, sum1])
    for chain in (sum0, sum1):
        while not chain.done():
            chain.advance()
            line.meet([chain])
    weight_grad, gain_part = owned_sums((sum0, sum1), weight_rows, pair, owned)
    gain_grad = line.arrived(gain_part)[0]
    there = line.arrived(swap(gain_grad, axis))
    gain_grad = jnp.where(first, jnp.concatenate([gain_grad, there]), jnp.concatenate([there, gain_grad]))
    others = [
        lax.ppermute(gain_grad, axis, [(i, (i + 2 * k) % count) for i in range(count)]) for k in range(1, pairs)
    ]
    u0, u1 = line.arrived(u0, u1)
    upstream_grad = line.arrived(jnp.concatenate([u0, u1], axis=0))
    features = jnp.stack([gain_grad, *line.arrived(*others)])
    gain_grad = features[lax.rem(pair - jnp.arange(pairs) + pairs, pairs)].reshape(-1) / line.token
    return (upstream_grad[None], weight_grad[None], gain_grad[None])


def solution(mesh):
    placed = (
        P("section", "fsdp", None),
        P("section", "fsdp", None),
        P("section", "fsdp", None),
        P("section", "fsdp", None),
        P("section", "fsdp", None),
        P("section", "fsdp", None),
        P("section", None),
    )
    return jax.shard_map(
        local,
        mesh=mesh,
        in_specs=placed,
        out_specs=(P("section", "fsdp", None), P("section", "fsdp", None), P("section", None)),
        check_vma=False,
    )
```

time: 225 us -> 221 us (0.982)
  starting transfers between devices: 58.9 us -> 91.4 us
  waiting for transfers between devices: 82.9 us -> 53.4 us
  Pallas kernels: 55.9 us -> 45 us
  other arithmetic: 9.35 us -> 12.1 us
    ppermute x14, waiting for transfers between devices: 62.1 us -> 38.7 us  [hop(): lax.ppermute(value, axis, [(2 * o + q, 2 * (o + step) + q) for o in sourc...]
    ppermute x14, starting transfers between devices: 34.8 us -> 52.3 us  [hop(): lax.ppermute(value, axis, [(2 * o + q, 2 * (o + step) + q) for o in sourc...]
    ppermute x5 -> x12, starting transfers between devices: 6.01 us -> 22.7 us  [the longest x4 8.51 us: swap_in_layers(): lax.ppermute(value, ('section', axis), [(k * count + i, k * count + (i ^...]
    pallas_call x14 -> x15, Pallas kernels: 51.3 us -> 42.3 us  [the longest x3 11.6 us: transpose_product(): pl.pallas_call(kernel, in_specs=[VMEM] * (len(pieces) + 1), out_specs=VME...]
    ppermute x6 -> x3, waiting for transfers between devices: 11 us -> 4.25 us  [swap(): return lax.ppermute(value, axis, [(i, i ^ 1) for i in range(count)])]
    select_n x3 -> x7, other arithmetic: 0.62 us -> 6.19 us  [the longest x2 4.53 us: local(): jnp.where(stands_in, there[:, edges[i]:edges[i + 1]], seconds[i])]
    concatenate x0 -> x2, other arithmetic: none -> 5.15 us  [the longest x1 3.11 us: local(): upstream_grad = line.arrived(jnp.concatenate([u0, u1], axis=0))]
    add x2 -> x0, other arithmetic: 3.89 us -> none  [total(): return own.astype(F32) + sum((came.astype(F32) for came in self.flying))]
  transfers between devices with their start and end apart: 27 -> 31, of which waited for: 12 -> 8; matrix products, arithmetic and copies ran while one was open for 4% -> 8% of each run, Pallas kernels for 23% -> 21%
where the time goes in v2:
time: 221 us; the launch traced here: 219 us
  starting transfers between devices  91.4 us (41%)
  waiting for transfers between devices  53.4 us (24%)
  Pallas kernels  45 us (20%)
  local copies, waits for them, and re-layouts  15.7 us (7%)
  other arithmetic  12.1 us (5%)
    ppermute x14, starting transfers between devices, hop(): lax.ppermute(value, axis, [(2 * o + q, 2 * (o + step) + q) for o in sourc...  52.3 us
    ppermute x14, waiting for transfers between devices, hop(): lax.ppermute(value, axis, [(2 * o + q, 2 * (o + step) + q) for o in sourc...  38.7 us
    pallas_call x3, Pallas kernels, transpose_product(): pl.pallas_call(kernel, in_specs=[VMEM] * (len(pieces) + 1), out_specs=VME...  11.6 us
    pallas_call x2, Pallas kernels, weight_term(): pl.pallas_call(kernel, in_specs=[ANY] * len(operands), out_specs=[VMEM] *...  10.5 us
    unnamed x63, local copies, waits for them, and re-layouts  10.1 us
    ppermute x2, starting transfers between devices, advance(): self.flying = [lax.ppermute(send, self.axis, route)]  9.88 us
    ppermute x3, waiting for transfers between devices, to_stand_in(): return lax.ppermute(own, 'section', [(helped, 0)])  8.62 us
    ppermute x4, starting transfers between devices, swap_in_layers(): lax.ppermute(value, ('section', axis), [(k * count + i, k * count + (i ^...  8.51 us
  transfers between devices with their start and end apart: 31, of which 8 were waited for; matrix products, arithmetic and copies ran while one was open for 8% of the time, Pallas kernels for 21%

profile of v2, /device:TPU:0, one launch (start us, length us, event | category | flops | bytes accessed | tf_op | source)
XLA Modules:
  0.0 219.0 jit_solution(2793464070990823178)
XLA Ops:
  3.2 5.0 %shard_map.94 = (bf16[1024,512]{1,0:T(8,128)(2,1)}, bf16[512,2304]{1,0:T(8,128)(2,1)}) custom-call(s32[1]{0:T(128)} %bitcast.side_ref, f32[1,2048]{1,0:T(1,128)} %gain_ref.3, bf16[512,2048]{1,0:T(8,128)(2,1)} %bitcast.55, bf16[512,3072]{1,0:T(8,128)(2,1)} %bitcast.43), custom_call_target="tpu_custom_call" | custom-call | flops 1 | bytes 1 | tf_op jit(solution)/shard_map/pallas_call | solution.py:178
  8.3 3.0 %collective-permute-start = (bf16[512,2304]{1,0:T(8,128)(2,1)}, bf16[512,2304]{1,0:T(8,128)(2,1)}, u32[]{:S(2)}, u32[]{:S(2)}) collective-permute-start(bf16[512,2304]{1,0:T(8,128)(2,1)} %get-tuple-element.104), channel_id=1, source_target_pairs={{0,1},{1,0},{2,3},{3,2},{4,5},{5,4},{6,7},{7,6},{8,9},{9,8},{10,11... | collective-permute-start | bytes 7077896 | tf_op jit(solution)/shard_map/ppermute | solution.py:22
  11.3 1.9 slice_bitcast_fusion
  13.2 1.8 slice_bitcast_fusion.2
  15.0 8.6 %collective-permute-done.2 = f32[2048]{0:T(1024)S(1)} collective-permute-done((f32[2048]{0:T(1024)}, f32[2048]{0:T(1024)S(1)}, u32[]{:S(2)}, u32[]{:S(2)}) %collective-permute-start.2) | collective-permute-done | bytes 8224 | tf_op jit(solution)/shard_map/ppermute | solution.py:421
  23.6 1.6 broadcast_select_fusion.shard_ref
  25.2 5.7 %collective-permute-start.3 = (bf16[256,3072]{1,0:T(8,128)(2,1)S(1)}, bf16[256,3072]{1,0:T(8,128)(2,1)}, u32[]{:S(2)}, u32[]{:S(2)}) collective-permute-start(bf16[256,3072]{1,0:T(8,128)(2,1)S(1)} %broadcast_select_fusion.shard_ref), channel_id=1, source_target_pairs={{0,2},{1,3},{2,4},{3,5},{4,6},{5,7},{8,10},{9,11},{10,12},{11,13},... | collective-permute-start | bytes 4718600 | tf_op jit(solution)/shard_map/ppermute | solution.py:26
  32.3 2.0 pad_maximum_fusion
  34.4 1.4 collective-permute-start.6
  35.8 16.8 %collective-permute-done.3.refs_0_ = bf16[256,3072]{1,0:T(8,128)(2,1)} collective-permute-done((bf16[256,3072]{1,0:T(8,128)(2,1)S(1)}, bf16[256,3072]{1,0:T(8,128)(2,1)}, u32[]{:S(2)}, u32[]{:S(2)}) %collective-permute-start.3) | collective-permute-done | bytes 1572896 | tf_op jit(solution)/shard_map/ppermute | solution.py:26
  52.5 9.7 %collective-permute-done.4.refs_3_ = bf16[256,3072]{1,0:T(8,128)(2,1)} collective-permute-done((bf16[256,3072]{1,0:T(8,128)(2,1)S(1)}, bf16[256,3072]{1,0:T(8,128)(2,1)}, u32[]{:S(2)}, u32[]{:S(2)}) %collective-permute-start.4) | collective-permute-done | bytes 1572896 | tf_op jit(solution)/shard_map/ppermute | solution.py:26
  62.3 1.8 collective-permute-start.8
  66.7 1.5 collective-permute-start.5
  68.2 1.9 copy-done.3
  71.4 4.6 %shard_map.95 = (bf16[1024,512]{1,0:T(8,128)(2,1)S(1)}, bf16[1024,1280]{1,0:T(8,128)(2,1)S(1)}) custom-call(bf16[1024,512]{1,0:T(8,128)(2,1)S(1)} %copy-done.10, bf16[512,3072]{1,0:T(8,128)(2,1)S(1)} %bitcast.45, bf16[512,2304]{1,0:T(8,128)(2,1)} %collective-permute-done.got_any), custom_call_target="tpu_custom_call" | custom-call | flops 1 | bytes 1 | tf_op jit(solution)/shard_map/pallas_call | solution.py:359
  78.0 4.6 %collective-permute-start.7 = (bf16[256,1280]{1,0:T(8,128)(2,1)}, bf16[256,1280]{1,0:T(8,128)(2,1)S(1)}, u32[]{:S(2)}, u32[]{:S(2)}) collective-permute-start(bf16[256,1280]{1,0:T(8,128)(2,1)} %shard_map.96), channel_id=1, source_target_pairs={{0,2},{1,3},{6,4},{7,5},{8,10},{9,11},{14,12},{15,13},{16,18},{17,... | collective-permute-start | bytes 1966088 | tf_op jit(solution)/shard_map/ppermute | solution.py:81
  82.7 8.9 %collective-permute-done.9.refs_4_ = bf16[256,3072]{1,0:T(8,128)(2,1)} collective-permute-done((bf16[256,3072]{1,0:T(8,128)(2,1)}, bf16[256,3072]{1,0:T(8,128)(2,1)}, u32[]{:S(2)}, u32[]{:S(2)}) %collective-permute-start.9) | collective-permute-done | bytes 1572896 | tf_op jit(solution)/shard_map/ppermute | solution.py:26
  91.6 1.8 collective-permute-done.7.refs_0_.refs_1_
  94.6 4.3 %collective-permute-start.12 = (bf16[256,1280]{1,0:T(8,128)(2,1)S(1)}, bf16[256,1280]{1,0:T(8,128)(2,1)S(1)}, u32[]{:S(2)}, u32[]{:S(2)}) collective-permute-start(bf16[256,1280]{1,0:T(8,128)(2,1)S(1)} %get-tuple-element.128), channel_id=1, source_target_pairs={{0,2},{1,3},{2,4},{3,5},{8,10},{9,11},{10,12},{11,13},{16,18},{17,... | collective-permute-start | bytes 1966088 | tf_op jit(solution)/shard_map/ppermute | solution.py:26
  99.0 1.8 collective-permute-start.10
  102.1 2.7 %collective-permute-done.5.got_any = bf16[512,1792]{1,0:T(8,128)(2,1)} collective-permute-done((bf16[512,1792]{1,0:T(8,128)(2,1)}, bf16[512,1792]{1,0:T(8,128)(2,1)}, u32[]{:S(2)}, u32[]{:S(2)}) %collective-permute-start.5) | collective-permute-done | bytes 1835040 | tf_op jit(solution)/shard_map/ppermute | solution.py:22
  104.8 1.8 collective-permute-start.14
  109.1 5.9 %shard_map.101.term_any.refs_1_ = bf16[1024,1792]{1,0:T(8,128)(2,1)S(1)} custom-call(bf16[1024,512]{1,0:T(8,128)(2,1)S(1)} %copy-done.11, bf16[512,3072]{1,0:T(8,128)(2,1)S(1)} %bitcast.46, bf16[512,1792]{1,0:T(8,128)(2,1)} %collective-permute-done.5.got_any, bf16[1024,512]{1,0:T(8,128)(2,1)S(1)} %copy-done.15), custom_call_target="tpu_custom_call" | custom-call | flops 1 | bytes 1 | tf_op jit(solution)/shard_map/pallas_call | solution.py:359
  117.3 5.3 %collective-permute-start.15 = (bf16[256,1792]{1,0:T(8,128)(2,1)}, bf16[256,1792]{1,0:T(8,128)(2,1)S(1)}, u32[]{:S(2)}, u32[]{:S(2)}) collective-permute-start(bf16[256,1792]{1,0:T(8,128)(2,1)} %shard_map.102), channel_id=1, source_target_pairs={{0,2},{1,3},{6,4},{7,5},{8,10},{9,11},{14,12},{15,13},{16,18},{17,... | collective-permute-start | bytes 2752520 | tf_op jit(solution)/shard_map/ppermute | solution.py:81
  122.6 2.7 %slice_select_fusion.refs_1_ = bf16[256,3072]{1,0:T(8,128)(2,1)} fusion(bf16[256,7168]{1,0:T(8,128)(2,1)} %collective-permute-done.6, pred[]{:T(512)S(6)} %eq.6, bf16[1,512,3072]{2,1,0:T(8,128)(2,1)S(1)} %copy-done.22), kind=kLoop, calls=%fused_computation.3 | loop fusion | flops 786432 | bytes 4718593 | tf_op jit(solution)/shard_map/jit(_where)/select_n | solution.py:466
  126.2 3.4 %collective-permute-start.19 = (bf16[256,3072]{1,0:T(8,128)(2,1)}, bf16[256,3072]{1,0:T(8,128)(2,1)}, u32[]{:S(2)}, u32[]{:S(2)}) collective-permute-start(bf16[256,3072]{1,0:T(8,128)(2,1)} %slice_select_fusion.refs_1_), channel_id=1, source_target_pairs={{0,1},{1,0},{2,3},{3,2},{4,5},{5,4},{6,7},{7,6},{8,9},{9,8},{10,11... | collective-permute-start | bytes 4718600 | tf_op jit(solution)/shard_map/ppermute | solution.py:424
  133.3 2.7 %shard_map.99.refs_2_.refs_1_ = bf16[1024,3072]{1,0:T(8,128)(2,1)S(1)} custom-call(s32[1]{0:T(128)} %bitcast.12.pair_ref, bf16[256,3072]{1,0:T(8,128)(2,1)S(1)} %copy-done.6, bf16[256,3072]{1,0:T(8,128)(2,1)} %collective-permute-done.3.refs_0_, bf16[256,3072]{1,0:T(8,128)(2,1)} %collective-permute-done.8.refs_1_, ...), custom_call_target="tpu_custom_call" | custom-call | flops 1 | bytes 1 | tf_op jit(solution)/shard_map/pallas_call | solution.py:136
  136.1 5.0 %shard_map.100.mine_ref = f32[512,1024]{1,0:T(8,128)S(1)} custom-call(bf16[256,3072]{1,0:T(8,128)(2,1)S(1)} %copy-done.9, bf16[256,3072]{1,0:T(8,128)(2,1)} %slice_select_fusion.refs_1_, bf16[1024,3072]{1,0:T(8,128)(2,1)S(1)} %shard_map.99.refs_2_.refs_1_), custom_call_target="tpu_custom_call" | custom-call | flops 1 | bytes 1 | tf_op jit(solution)/shard_map/pallas_call | solution.py:237
  141.2 1.4 shard_map.103
  142.6 7.4 %collective-permute-start.20 = (bf16[256,1792]{1,0:T(8,128)(2,1)S(1)}, bf16[256,1792]{1,0:T(8,128)(2,1)S(1)}, u32[]{:S(2)}, u32[]{:S(2)}) collective-permute-start(bf16[256,1792]{1,0:T(8,128)(2,1)S(1)} %get-tuple-element.156), channel_id=1, source_target_pairs={{0,2},{1,3},{2,4},{3,5},{8,10},{9,11},{10,12},{11,13},{16,18},{17,... | collective-permute-start | bytes 2752520 | tf_op jit(solution)/shard_map/ppermute | solution.py:26
  150.7 10.8 %collective-permute-start.17 = (bf16[256,1280]{1,0:T(8,128)(2,1)S(1)}, bf16[256,1280]{1,0:T(8,128)(2,1)S(1)}, u32[]{:S(2)}, u32[]{:S(2)}) collective-permute-start(bf16[256,1280]{1,0:T(8,128)(2,1)S(1)} %get-tuple-element.153), channel_id=1, source_target_pairs={{0,2},{1,3},{2,4},{3,5},{4,6},{5,7},{8,10},{9,11},{10,12},{11,13},... | collective-permute-start | bytes 1966088 | tf_op jit(solution)/shard_map/ppermute | solution.py:26
  162.9 3.2 %shard_map.104 = bf16[256,1024]{1,0:T(8,128)(2,1)S(1)} custom-call(bf16[256,3072]{1,0:T(8,128)(2,1)} %collective-permute-done.14.refs_0_, bf16[1024,3072]{1,0:T(8,128)(2,1)S(1)} %shard_map.99.refs_2_.refs_1_), custom_call_target="tpu_custom_call" | custom-call | flops 1 | bytes 1 | tf_op jit(solution)/shard_map/pallas_call | solution.py:237
  166.8 1.4 shard_map.105
  168.3 3.4 %shard_map.106 = bf16[256,1024]{1,0:T(8,128)(2,1)S(1)} custom-call(bf16[256,3072]{1,0:T(8,128)(2,1)} %collective-permute-done.19.refs_0_, bf16[1024,3072]{1,0:T(8,128)(2,1)S(1)} %shard_map.99.refs_2_.refs_1_), custom_call_target="tpu_custom_call" | custom-call | flops 1 | bytes 1 | tf_op jit(solution)/shard_map/pallas_call | solution.py:237
  171.7 2.6 %collective-permute-start.23 = (bf16[256,1024]{1,0:T(8,128)(2,1)S(1)}, bf16[256,1024]{1,0:T(8,128)(2,1)S(1)}, u32[]{:S(2)}, u32[]{:S(2)}) collective-permute-start(bf16[256,1024]{1,0:T(8,128)(2,1)S(1)} %shard_map.106), channel_id=1, source_target_pairs={{0,1},{1,0},{2,3},{3,2},{4,5},{5,4},{6,7},{7,6},{8,9},{9,8},{10,11... | collective-permute-start | bytes 1572872 | tf_op jit(solution)/shard_map/ppermute | solution.py:424
  174.3 12.4 %collective-permute-start.25 = (bf16[256,1792]{1,0:T(8,128)(2,1)S(1)}, bf16[256,1792]{1,0:T(8,128)(2,1)S(1)}, u32[]{:S(2)}, u32[]{:S(2)}) collective-permute-start(bf16[256,1792]{1,0:T(8,128)(2,1)S(1)} %get-tuple-element.180), channel_id=1, source_target_pairs={{0,2},{1,3},{2,4},{3,5},{4,6},{5,7},{8,10},{9,11},{10,12},{11,13},... | collective-permute-start | bytes 2752520 | tf_op jit(solution)/shard_map/ppermute | solution.py:26
  188.1 1.8 slice_select_fusion.1
  189.9 2.2 %shard_map.107 = bf16[256,2048]{1,0:T(8,128)(2,1)} custom-call(s32[1]{0:T(128)} %bitcast.side_ref, f32[512,1024]{1,0:T(8,128)S(1)} %shard_map.100.mine_ref, bf16[256,1024]{1,0:T(8,128)(2,1)S(1)} %collective-permute-done.16.theirs_ref, bf16[256,2048]{1,0:T(8,128)(2,1)S(1)} %copy-done.13, bf16[256,2048]{1,0:T(8,128)(2,1)S(1)} %copy-done.12, ...), custom_call_target="tpu_custom_call" | custom-call | flops 1 | bytes 1 | tf_op jit(solution)/shard_map/pallas_call | solution.py:271
  193.5 2.2 %shard_map.108 = bf16[256,2048]{1,0:T(8,128)(2,1)} custom-call(s32[1]{0:T(128)} %bitcast.side_ref, f32[512,1024]{1,0:T(8,128)S(1)} %shard_map.100.mine_ref, bf16[256,1024]{1,0:T(8,128)(2,1)S(1)} %collective-permute-done.23.theirs_ref, bf16[256,2048]{1,0:T(8,128)(2,1)S(1)} %get-tuple-element.204.rows_ref, bf16[256,2048]{1,0:T(8,128)(2,1)S(1)} %get-tuple-element.203.resid_ref, ...), custom_call_target="tpu_custom_call" | custom-call | flops 1 | bytes 1 | tf_op jit(solution)/shard_map/pallas_call | solution.py:271
  195.7 3.0 %collective-permute-start.24 = (bf16[256,2048]{1,0:T(8,128)(2,1)}, bf16[256,2048]{1,0:T(8,128)(2,1)}, u32[]{:S(2)}, u32[]{:S(2)}) collective-permute-start(bf16[256,2048]{1,0:T(8,128)(2,1)} %shard_map.108), channel_id=1, source_target_pairs={{8,0},{0,8},{24,16},{9,1},{1,9},{25,17},{10,2},{2,10},{26,18},{11,... | collective-permute-start | bytes 3145736 | tf_op jit(solution)/shard_map/ppermute | solution.py:441
  198.7 3.3 %collective-permute-done.26.refs_5_ = bf16[256,1792]{1,0:T(8,128)(2,1)S(1)} collective-permute-done((bf16[256,1792]{1,0:T(8,128)(2,1)S(1)}, bf16[256,1792]{1,0:T(8,128)(2,1)S(1)}, u32[]{:S(2)}, u32[]{:S(2)}) %collective-permute-start.26) | collective-permute-done | bytes 917536 | tf_op jit(solution)/shard_map/ppermute | solution.py:26
  202.0 3.1 %shard_map.109 = (f32[256,3072]{1,0:T(8,128)}, f32[1,256]{1,0:T(1,128)S(1)}) custom-call(s32[1]{0:T(128)} %bitcast.12.pair_ref, bf16[256,3072]{1,0:T(8,128)(2,1)S(1)} %bitcast.48, bf16[1024,1280]{1,0:T(8,128)(2,1)S(1)} %get-tuple-element.115.term_any.refs_0_, bf16[1024,1792]{1,0:T(8,128)(2,1)S(1)} %copy-done.1, ...), custom_call_target="tpu_custom_call" | custom-call | flops 1 | bytes 1 | tf_op jit(solution)/shard_map/pallas_call | solution.py:313
  205.1 2.1 collective-permute-start.27
  207.2 1.5 collective-permute-done.27
  208.8 1.5 collective-permute-start.28
  210.3 1.4 collective-permute-start.29
  211.8 2.9 %collective-permute-start.30 = (f32[512]{0:T(512)S(1)}, f32[512]{0:T(512)S(1)}, u32[]{:S(2)}, u32[]{:S(2)}) collective-permute-start(f32[512]{0:T(512)S(1)} %maximum_select_fusion), channel_id=1, source_target_pairs={{0,6},{1,7},{2,0},{3,1},{4,2},{5,3},{6,4},{7,5},{8,14},{9,15},{10,... | collective-permute-start | bytes 6152 | tf_op jit(solution)/shard_map/ppermute | solution.py:503
  214.6 3.1 %pad_maximum_fusion.1 = bf16[512,2048]{1,0:T(8,128)(2,1)} fusion(bf16[256,2048]{1,0:T(8,128)(2,1)} %collective-permute-done.24, bf16[256,2048]{1,0:T(8,128)(2,1)} %collective-permute-done.22), kind=kLoop, calls=%fused_computation.2 | loop fusion | flops 4194304 | bytes 4194304 | tf_op jit(solution)/shard_map/concatenate | solution.py:506
  (111 shorter events, 28.4 us)
Async XLA Ops:
  0.6 23.0 %collective-permute-start.1 = (bf16[256,3072]{1,0:T(8,128)(2,1)}, bf16[256,3072]{1,0:T(8,128)(2,1)}, u32[]{:S(2)}, u32[]{:S(2)}) collective-permute-start(bf16[256,3072]{1,0:T(8,128)(2,1)} %bitcast.47), channel_id=1, source_target_pairs={{16,0},{17,1},{18,2},{19,3},{20,4},{21,5},{22,6},{23,7}} | collective-permute-start | bytes 4718600 | tf_op jit(solution)/shard_map/ppermute | solution.py:421
  1.9 21.7 %collective-permute-start.2 = (f32[2048]{0:T(1024)}, f32[2048]{0:T(1024)S(1)}, u32[]{:S(2)}, u32[]{:S(2)}) collective-permute-start(f32[2048]{0:T(1024)} %bitcast.49), channel_id=1, source_target_pairs={{16,0},{17,1},{18,2},{19,3},{20,4},{21,5},{22,6},{23,7}} | collective-permute-start | bytes 24584 | tf_op jit(solution)/shard_map/ppermute | solution.py:421
  3.2 8.1 %copy-start.21 = (bf16[1,512,3072]{2,1,0:T(8,128)(2,1)S(1)}, bf16[1,512,3072]{2,1,0:T(8,128)(2,1)}, u32[]{:S(2)}) copy-start(bf16[1,512,3072]{2,1,0:T(8,128)(2,1)} %param.9) | copy-start | bytes 9437188
  8.3 60.0 %collective-permute-start = (bf16[512,2304]{1,0:T(8,128)(2,1)}, bf16[512,2304]{1,0:T(8,128)(2,1)}, u32[]{:S(2)}, u32[]{:S(2)}) collective-permute-start(bf16[512,2304]{1,0:T(8,128)(2,1)} %get-tuple-element.104), channel_id=1, source_target_pairs={{0,1},{1,0},{2,3},{3,2},{4,5},{5,4},{6,7},{7,6},{8,9},{9,8},{10,11... | collective-permute-start | bytes 7077896 | tf_op jit(solution)/shard_map/ppermute | solution.py:22
  13.2 10.4 %copy-start.7 = (bf16[1,256,3072]{2,1,0:T(8,128)(2,1)S(1)}, bf16[1,256,3072]{2,1,0:T(8,128)(2,1)}, u32[]{:S(2)}) copy-start(bf16[1,256,3072]{2,1,0:T(8,128)(2,1)} %param.12) | copy-start | bytes 4718596
  15.0 17.3 %copy-start.23 = (bf16[256,3072]{1,0:T(8,128)(2,1)S(1)}, bf16[256,3072]{1,0:T(8,128)(2,1)}, u32[]{:S(2)}) copy-start(bf16[256,3072]{1,0:T(8,128)(2,1)} %get-tuple-element.205) | copy-start | bytes 4718596
  15.0 17.3 %copy-start.28 = (bf16[256,2048]{1,0:T(8,128)(2,1)S(1)}, bf16[256,2048]{1,0:T(8,128)(2,1)}, u32[]{:S(2)}) copy-start(bf16[256,2048]{1,0:T(8,128)(2,1)} %get-tuple-element.211) | copy-start | bytes 3145732
  25.2 9.1 %copy-start.5 = (bf16[256,3072]{1,0:T(8,128)(2,1)}, bf16[256,3072]{1,0:T(8,128)(2,1)S(1)}, u32[]{:S(2)}) copy-start(bf16[256,3072]{1,0:T(8,128)(2,1)S(1)} %broadcast_select_fusion.shard_ref) | copy-start | bytes 4718596
  25.2 27.3 %collective-permute-start.3 = (bf16[256,3072]{1,0:T(8,128)(2,1)S(1)}, bf16[256,3072]{1,0:T(8,128)(2,1)}, u32[]{:S(2)}, u32[]{:S(2)}) collective-permute-start(bf16[256,3072]{1,0:T(8,128)(2,1)S(1)} %broadcast_select_fusion.shard_ref), channel_id=1, source_target_pairs={{0,2},{1,3},{2,4},{3,5},{4,6},{5,7},{8,10},{9,11},{10,12},{11,13},... | collective-permute-start | bytes 4718600 | tf_op jit(solution)/shard_map/ppermute | solution.py:26
  31.0 31.3 %collective-permute-start.4 = (bf16[256,3072]{1,0:T(8,128)(2,1)S(1)}, bf16[256,3072]{1,0:T(8,128)(2,1)}, u32[]{:S(2)}, u32[]{:S(2)}) collective-permute-start(bf16[256,3072]{1,0:T(8,128)(2,1)S(1)} %broadcast_select_fusion.shard_ref), channel_id=1, source_target_pairs={{2,0},{3,1},{4,2},{5,3},{6,4},{7,5},{10,8},{11,9},{12,10},{13,11},... | collective-permute-start | bytes 4718600 | tf_op jit(solution)/shard_map/ppermute | solution.py:26
  32.3 33.1 %copy-start.2 = (bf16[1,512,3072]{2,1,0:T(8,128)(2,1)S(1)}, bf16[1,512,3072]{2,1,0:T(8,128)(2,1)}, u32[]{:S(2)}) copy-start(bf16[1,512,3072]{2,1,0:T(8,128)(2,1)} %param.11) | copy-start | bytes 9437188
  34.4 72.3 %collective-permute-start.6 = (bf16[256,7168]{1,0:T(8,128)(2,1)}, bf16[256,7168]{1,0:T(8,128)(2,1)}, u32[]{:S(2)}, u32[]{:S(2)}) collective-permute-start(bf16[256,7168]{1,0:T(8,128)(2,1)} %pad_maximum_fusion), channel_id=1, source_target_pairs={{16,0},{17,1},{18,2},{19,3},{20,4},{21,5},{22,6},{23,7}} | collective-permute-start | bytes 11010056 | tf_op jit(solution)/shard_map/ppermute | solution.py:421
  62.3 20.4 %collective-permute-start.8 = (bf16[256,3072]{1,0:T(8,128)(2,1)}, bf16[256,3072]{1,0:T(8,128)(2,1)}, u32[]{:S(2)}, u32[]{:S(2)}) collective-permute-start(bf16[256,3072]{1,0:T(8,128)(2,1)} %collective-permute-done.3.refs_0_), channel_id=1, source_target_pairs={{2,4},{3,5},{4,6},{5,7},{10,12},{11,13},{12,14},{13,15},{18,20},{1... | collective-permute-start | bytes 4718600 | tf_op jit(solution)/shard_map/ppermute | solution.py:26
  64.1 27.5 %collective-permute-start.9 = (bf16[256,3072]{1,0:T(8,128)(2,1)}, bf16[256,3072]{1,0:T(8,128)(2,1)}, u32[]{:S(2)}, u32[]{:S(2)}) collective-permute-start(bf16[256,3072]{1,0:T(8,128)(2,1)} %collective-permute-done.4.refs_3_), channel_id=1, source_target_pairs={{2,0},{3,1},{4,2},{5,3},{10,8},{11,9},{12,10},{13,11},{18,16},{19,... | collective-permute-start | bytes 4718600 | tf_op jit(solution)/shard_map/ppermute | solution.py:26
  66.7 38.0 %collective-permute-start.5 = (bf16[512,1792]{1,0:T(8,128)(2,1)}, bf16[512,1792]{1,0:T(8,128)(2,1)}, u32[]{:S(2)}, u32[]{:S(2)}) collective-permute-start(bf16[512,1792]{1,0:T(8,128)(2,1)} %slice.50), channel_id=1, source_target_pairs={{0,1},{1,0},{2,3},{3,2},{4,5},{5,4},{6,7},{7,6},{8,9},{9,8},{10,11... | collective-permute-start | bytes 5505032 | tf_op jit(solution)/shard_map/ppermute | solution.py:22
  78.0 15.3 %collective-permute-start.7 = (bf16[256,1280]{1,0:T(8,128)(2,1)}, bf16[256,1280]{1,0:T(8,128)(2,1)S(1)}, u32[]{:S(2)}, u32[]{:S(2)}) collective-permute-start(bf16[256,1280]{1,0:T(8,128)(2,1)} %shard_map.96), channel_id=1, source_target_pairs={{0,2},{1,3},{6,4},{7,5},{8,10},{9,11},{14,12},{15,13},{16,18},{17,... | collective-permute-start | bytes 1966088 | tf_op jit(solution)/shard_map/ppermute | solution.py:81
  82.6 24.0 %copy-start.4 = (bf16[1,512,3072]{2,1,0:T(8,128)(2,1)S(1)}, bf16[1,512,3072]{2,1,0:T(8,128)(2,1)}, u32[]{:S(2)}) copy-start(bf16[1,512,3072]{2,1,0:T(8,128)(2,1)} %param.11) | copy-start | bytes 9437188
  94.6 22.7 %collective-permute-start.12 = (bf16[256,1280]{1,0:T(8,128)(2,1)S(1)}, bf16[256,1280]{1,0:T(8,128)(2,1)S(1)}, u32[]{:S(2)}, u32[]{:S(2)}) collective-permute-start(bf16[256,1280]{1,0:T(8,128)(2,1)S(1)} %get-tuple-element.128), channel_id=1, source_target_pairs={{0,2},{1,3},{2,4},{3,5},{8,10},{9,11},{10,12},{11,13},{16,18},{17,... | collective-permute-start | bytes 1966088 | tf_op jit(solution)/shard_map/ppermute | solution.py:26
  99.0 34.3 %collective-permute-start.10 = (bf16[256,3072]{1,0:T(8,128)(2,1)}, bf16[256,3072]{1,0:T(8,128)(2,1)}, u32[]{:S(2)}, u32[]{:S(2)}) collective-permute-start(bf16[256,3072]{1,0:T(8,128)(2,1)} %collective-permute-done.8.refs_1_), channel_id=1, source_target_pairs={{4,6},{5,7},{12,14},{13,15},{20,22},{21,23},{28,30},{29,31}} | collective-permute-start | bytes 4718600 | tf_op jit(solution)/shard_map/ppermute | solution.py:26
  100.8 32.5 %collective-permute-start.11 = (bf16[256,3072]{1,0:T(8,128)(2,1)}, bf16[256,3072]{1,0:T(8,128)(2,1)}, u32[]{:S(2)}, u32[]{:S(2)}) collective-permute-start(bf16[256,3072]{1,0:T(8,128)(2,1)} %collective-permute-done.9.refs_4_), channel_id=1, source_target_pairs={{2,0},{3,1},{10,8},{11,9},{18,16},{19,17},{26,24},{27,25}} | collective-permute-start | bytes 4718600 | tf_op jit(solution)/shard_map/ppermute | solution.py:26
  104.8 56.7 %collective-permute-start.14 = (bf16[256,3072]{1,0:T(8,128)(2,1)}, bf16[256,3072]{1,0:T(8,128)(2,1)}, u32[]{:S(2)}, u32[]{:S(2)}) collective-permute-start(bf16[256,3072]{1,0:T(8,128)(2,1)} %get-tuple-element.111.refs_0_), channel_id=1, source_target_pairs={{8,9},{9,8},{10,11},{11,10},{12,13},{13,12},{14,15},{15,14},{16,17... | collective-permute-start | bytes 4718600 | tf_op jit(solution)/shard_map/ppermute | solution.py:424
  115.0 7.6 %copy-start.22 = (bf16[1,512,3072]{2,1,0:T(8,128)(2,1)S(1)}, bf16[1,512,3072]{2,1,0:T(8,128)(2,1)}, u32[]{:S(2)}) copy-start(bf16[1,512,3072]{2,1,0:T(8,128)(2,1)} %param.9) | copy-start | bytes 9437188
  115.0 10.3 %collective-permute-start.13 = (bf16[256,1280]{1,0:T(8,128)(2,1)S(1)}, bf16[256,1280]{1,0:T(8,128)(2,1)S(1)}, u32[]{:S(2)}, u32[]{:S(2)}) collective-permute-start(bf16[256,1280]{1,0:T(8,128)(2,1)S(1)} %get-tuple-element.129), channel_id=1, source_target_pairs={{4,2},{5,3},{6,4},{7,5},{12,10},{13,11},{14,12},{15,13},{20,18},{2... | collective-permute-start | bytes 1966088 | tf_op jit(solution)/shard_map/ppermute | solution.py:26
  117.3 8.0 %copy-start.16 = (bf16[256,1280]{1,0:T(8,128)(2,1)}, bf16[256,1280]{1,0:T(8,128)(2,1)S(1)}, u32[]{:S(2)}) copy-start(bf16[256,1280]{1,0:T(8,128)(2,1)S(1)} %collective-permute-done.12.refs_0_) | copy-start | bytes 1966084
  117.3 23.9 %collective-permute-start.15 = (bf16[256,1792]{1,0:T(8,128)(2,1)}, bf16[256,1792]{1,0:T(8,128)(2,1)S(1)}, u32[]{:S(2)}, u32[]{:S(2)}) collective-permute-start(bf16[256,1792]{1,0:T(8,128)(2,1)} %shard_map.102), channel_id=1, source_target_pairs={{0,2},{1,3},{6,4},{7,5},{8,10},{9,11},{14,12},{15,13},{16,18},{17,... | collective-permute-start | bytes 2752520 | tf_op jit(solution)/shard_map/ppermute | solution.py:81
  126.2 42.1 %collective-permute-start.19 = (bf16[256,3072]{1,0:T(8,128)(2,1)}, bf16[256,3072]{1,0:T(8,128)(2,1)}, u32[]{:S(2)}, u32[]{:S(2)}) collective-permute-start(bf16[256,3072]{1,0:T(8,128)(2,1)} %slice_select_fusion.refs_1_), channel_id=1, source_target_pairs={{0,1},{1,0},{2,3},{3,2},{4,5},{5,4},{6,7},{7,6},{8,9},{9,8},{10,11... | collective-permute-start | bytes 4718600 | tf_op jit(solution)/shard_map/ppermute | solution.py:424
  136.1 5.0 %copy-start.1 = (bf16[1024,1792]{1,0:T(8,128)(2,1)S(1)}, bf16[1024,1792]{1,0:T(8,128)(2,1)}, u32[]{:S(2)}) copy-start(bf16[1024,1792]{1,0:T(8,128)(2,1)} %copy-done) | copy-start | bytes 11010052
  141.1 21.7 %copy-start.20 = (f32[1,2048]{1,0:T(1,128)S(1)}, f32[1,2048]{1,0:T(1,128)}, u32[]{:S(2)}) copy-start(f32[1,2048]{1,0:T(1,128)} %gain_ref.3) | copy-start | bytes 24580
  141.2 21.7 %copy-start.30 = (f32[2048]{0:T(1024)S(1)}, f32[2048]{0:T(1024)}, u32[]{:S(2)}) copy-start(f32[2048]{0:T(1024)} %copy-done.29) | copy-start | bytes 24580
  142.6 23.5 %collective-permute-start.20 = (bf16[256,1792]{1,0:T(8,128)(2,1)S(1)}, bf16[256,1792]{1,0:T(8,128)(2,1)S(1)}, u32[]{:S(2)}, u32[]{:S(2)}) collective-permute-start(bf16[256,1792]{1,0:T(8,128)(2,1)S(1)} %get-tuple-element.156), channel_id=1, source_target_pairs={{0,2},{1,3},{2,4},{3,5},{8,10},{9,11},{10,12},{11,13},{16,18},{17,... | collective-permute-start | bytes 2752520 | tf_op jit(solution)/shard_map/ppermute | solution.py:26
  150.0 16.8 %collective-permute-start.21 = (bf16[256,1792]{1,0:T(8,128)(2,1)S(1)}, bf16[256,1792]{1,0:T(8,128)(2,1)S(1)}, u32[]{:S(2)}, u32[]{:S(2)}) collective-permute-start(bf16[256,1792]{1,0:T(8,128)(2,1)S(1)} %get-tuple-element.157), channel_id=1, source_target_pairs={{4,2},{5,3},{6,4},{7,5},{12,10},{13,11},{14,12},{15,13},{20,18},{2... | collective-permute-start | bytes 2752520 | tf_op jit(solution)/shard_map/ppermute | solution.py:26
  150.7 36.0 %collective-permute-start.17 = (bf16[256,1280]{1,0:T(8,128)(2,1)S(1)}, bf16[256,1280]{1,0:T(8,128)(2,1)S(1)}, u32[]{:S(2)}, u32[]{:S(2)}) collective-permute-start(bf16[256,1280]{1,0:T(8,128)(2,1)S(1)} %get-tuple-element.153), channel_id=1, source_target_pairs={{0,2},{1,3},{2,4},{3,5},{4,6},{5,7},{8,10},{9,11},{10,12},{11,13},... | collective-permute-start | bytes 1966088 | tf_op jit(solution)/shard_map/ppermute | solution.py:26
  161.5 28.4 %collective-permute-start.18 = (bf16[256,1280]{1,0:T(8,128)(2,1)S(1)}, bf16[256,1280]{1,0:T(8,128)(2,1)S(1)}, u32[]{:S(2)}, u32[]{:S(2)}) collective-permute-start(bf16[256,1280]{1,0:T(8,128)(2,1)S(1)} %get-tuple-element.154), channel_id=1, source_target_pairs={{2,0},{3,1},{4,2},{5,3},{6,4},{7,5},{10,8},{11,9},{12,10},{13,11},... | collective-permute-start | bytes 1966088 | tf_op jit(solution)/shard_map/ppermute | solution.py:26
  166.1 23.8 %collective-permute-start.16 = (bf16[256,1024]{1,0:T(8,128)(2,1)S(1)}, bf16[256,1024]{1,0:T(8,128)(2,1)S(1)}, u32[]{:S(2)}, u32[]{:S(2)}) collective-permute-start(bf16[256,1024]{1,0:T(8,128)(2,1)S(1)} %shard_map.104), channel_id=1, source_target_pairs={{8,9},{9,8},{10,11},{11,10},{12,13},{13,12},{14,15},{15,14},{16,17... | collective-permute-start | bytes 1572872 | tf_op jit(solution)/shard_map/ppermute | solution.py:424
  168.3 19.8 %copy-start.25 = (bf16[1,512,2048]{2,1,0:T(8,128)(2,1)S(1)}, bf16[1,512,2048]{2,1,0:T(8,128)(2,1)}, u32[]{:S(2)}) copy-start(bf16[1,512,2048]{2,1,0:T(8,128)(2,1)} %param.8) | copy-start | bytes 6291460
  168.3 19.8 %copy-start.27 = (bf16[1,512,2048]{2,1,0:T(8,128)(2,1)S(1)}, bf16[1,512,2048]{2,1,0:T(8,128)(2,1)}, u32[]{:S(2)}) copy-start(bf16[1,512,2048]{2,1,0:T(8,128)(2,1)} %param.7) | copy-start | bytes 6291460
  171.7 18.2 %copy-start.12 = (bf16[256,2048]{1,0:T(8,128)(2,1)S(1)}, bf16[256,2048]{1,0:T(8,128)(2,1)}, u32[]{:S(2)}) copy-start(bf16[256,2048]{1,0:T(8,128)(2,1)} %get-tuple-element.207.resid_ref) | copy-start | bytes 3145732
  171.7 18.2 %copy-start.13 = (bf16[256,2048]{1,0:T(8,128)(2,1)S(1)}, bf16[256,2048]{1,0:T(8,128)(2,1)}, u32[]{:S(2)}) copy-start(bf16[256,2048]{1,0:T(8,128)(2,1)} %get-tuple-element.212.rows_ref) | copy-start | bytes 3145732
  171.7 21.7 %collective-permute-start.23 = (bf16[256,1024]{1,0:T(8,128)(2,1)S(1)}, bf16[256,1024]{1,0:T(8,128)(2,1)S(1)}, u32[]{:S(2)}, u32[]{:S(2)}) collective-permute-start(bf16[256,1024]{1,0:T(8,128)(2,1)S(1)} %shard_map.106), channel_id=1, source_target_pairs={{0,1},{1,0},{2,3},{3,2},{4,5},{5,4},{6,7},{7,6},{8,9},{9,8},{10,11... | collective-permute-start | bytes 1572872 | tf_op jit(solution)/shard_map/ppermute | solution.py:424
  174.3 24.4 %collective-permute-start.25 = (bf16[256,1792]{1,0:T(8,128)(2,1)S(1)}, bf16[256,1792]{1,0:T(8,128)(2,1)S(1)}, u32[]{:S(2)}, u32[]{:S(2)}) collective-permute-start(bf16[256,1792]{1,0:T(8,128)(2,1)S(1)} %get-tuple-element.180), channel_id=1, source_target_pairs={{0,2},{1,3},{2,4},{3,5},{4,6},{5,7},{8,10},{9,11},{10,12},{11,13},... | collective-permute-start | bytes 2752520 | tf_op jit(solution)/shard_map/ppermute | solution.py:26
  186.8 15.3 %collective-permute-start.26 = (bf16[256,1792]{1,0:T(8,128)(2,1)S(1)}, bf16[256,1792]{1,0:T(8,128)(2,1)S(1)}, u32[]{:S(2)}, u32[]{:S(2)}) collective-permute-start(bf16[256,1792]{1,0:T(8,128)(2,1)S(1)} %get-tuple-element.181), channel_id=1, source_target_pairs={{2,0},{3,1},{4,2},{5,3},{6,4},{7,5},{10,8},{11,9},{12,10},{13,11},... | collective-permute-start | bytes 2752520 | tf_op jit(solution)/shard_map/ppermute | solution.py:26
  192.1 22.5 %collective-permute-start.22 = (bf16[256,2048]{1,0:T(8,128)(2,1)}, bf16[256,2048]{1,0:T(8,128)(2,1)}, u32[]{:S(2)}, u32[]{:S(2)}) collective-permute-start(bf16[256,2048]{1,0:T(8,128)(2,1)} %shard_map.107), channel_id=1, source_target_pairs={{8,0},{16,8},{24,16},{9,1},{17,9},{25,17},{10,2},{18,10},{26,18},{... | collective-permute-start | bytes 3145736 | tf_op jit(solution)/shard_map/ppermute | solution.py:441
  193.4 8.6 %copy-start.8 = (bf16[1,256,3072]{2,1,0:T(8,128)(2,1)S(1)}, bf16[1,256,3072]{2,1,0:T(8,128)(2,1)}, u32[]{:S(2)}) copy-start(bf16[1,256,3072]{2,1,0:T(8,128)(2,1)} %param.12) | copy-start | bytes 4718596
  195.7 19.0 %collective-permute-start.24 = (bf16[256,2048]{1,0:T(8,128)(2,1)}, bf16[256,2048]{1,0:T(8,128)(2,1)}, u32[]{:S(2)}, u32[]{:S(2)}) collective-permute-start(bf16[256,2048]{1,0:T(8,128)(2,1)} %shard_map.108), channel_id=1, source_target_pairs={{8,0},{0,8},{24,16},{9,1},{1,9},{25,17},{10,2},{2,10},{26,18},{11,... | collective-permute-start | bytes 3145736 | tf_op jit(solution)/shard_map/ppermute | solution.py:441
  205.1 3.6 %collective-permute-start.27 = (f32[256]{0:T(256)S(1)}, f32[256]{0:T(256)S(1)}, u32[]{:S(2)}, u32[]{:S(2)}) collective-permute-start(f32[256]{0:T(256)S(1)} %bitcast.53), channel_id=1, source_target_pairs={{0,1},{1,0},{2,3},{3,2},{4,5},{5,4},{6,7},{7,6},{8,9},{9,8},{10,11... | collective-permute-start | bytes 3080 | tf_op jit(solution)/shard_map/ppermute | solution.py:22
  208.8 9.0 %collective-permute-start.28 = (f32[512]{0:T(512)S(1)}, f32[512]{0:T(512)S(1)}, u32[]{:S(2)}, u32[]{:S(2)}) collective-permute-start(f32[512]{0:T(512)S(1)} %maximum_select_fusion), channel_id=1, source_target_pairs={{0,2},{1,3},{2,4},{3,5},{4,6},{5,7},{6,0},{7,1},{8,10},{9,11},{10,... | collective-permute-start | bytes 6152 | tf_op jit(solution)/shard_map/ppermute | solution.py:503
  210.3 7.4 %collective-permute-start.29 = (f32[512]{0:T(512)S(1)}, f32[512]{0:T(512)S(1)}, u32[]{:S(2)}, u32[]{:S(2)}) collective-permute-start(f32[512]{0:T(512)S(1)} %maximum_select_fusion), channel_id=1, source_target_pairs={{0,4},{1,5},{2,6},{3,7},{4,0},{5,1},{6,2},{7,3},{8,12},{9,13},{10,... | collective-permute-start | bytes 6152 | tf_op jit(solution)/shard_map/ppermute | solution.py:503
  211.8 6.0 %collective-permute-start.30 = (f32[512]{0:T(512)S(1)}, f32[512]{0:T(512)S(1)}, u32[]{:S(2)}, u32[]{:S(2)}) collective-permute-start(f32[512]{0:T(512)S(1)} %maximum_select_fusion), channel_id=1, source_target_pairs={{0,6},{1,7},{2,0},{3,1},{4,2},{5,3},{6,4},{7,5},{8,14},{9,15},{10,... | collective-permute-start | bytes 6152 | tf_op jit(solution)/shard_map/ppermute | solution.py:503
  (14 other events, 30.0 us)

commit v3 on v2

--- a/solution.py
+++ b/solution.py
@@ -475,10 +475,10 @@
         gather.advance()
         line.meet([gather])
     weight_half = gather.whole()
-    direction_mine = line.arrived(transpose_product([now_first, now_second], weight_half, F32))
     part_inputs = [(rows_now[: bounds[1]], resid[: bounds[1]], gain), (rows_second, resid_second, gain_second)]
     line.meet([sum1])
     sum1.advance()
+    direction_mine = line.arrived(transpose_product([now_first, now_second], weight_half, F32))
     (g0,) = line.meet([], g0)
     r0 = back(g0, 0)
     line.meet([sum1])

time: 221 us -> 218 us (0.986)
  starting transfers between devices: 91.4 us -> 84.2 us
  waiting for transfers between devices: 53.4 us -> 58.7 us
    ppermute x14, starting transfers between devices: 52.3 us -> 44.3 us  [hop(): lax.ppermute(value, axis, [(2 * o + q, 2 * (o + step) + q) for o in sourc...]
    ppermute x2, waiting for transfers between devices: 1.76 us -> 7.04 us  [advance(): self.flying = [lax.ppermute(send, self.axis, route)]]
    unnamed x63 -> x59, local copies, waits for them, and re-layouts: 10.1 us -> 10.1 us
  transfers between devices with their start and end apart: 31 -> 31, of which waited for: 8 -> 9; matrix products, arithmetic and copies ran while one was open for 8% -> 8% of each run, Pallas kernels for 21% -> 21%
where the time goes in v3:
time: 218 us; the launch traced here: 217 us
  starting transfers between devices  84.2 us (39%)
  waiting for transfers between devices  58.7 us (27%)
  Pallas kernels  44.9 us (21%)
  local copies, waits for them, and re-layouts  15.7 us (7%)
  other arithmetic  12.2 us (6%)
    ppermute x14, starting transfers between devices, hop(): lax.ppermute(value, axis, [(2 * o + q, 2 * (o + step) + q) for o in sourc...  44.3 us
    ppermute x14, waiting for transfers between devices, hop(): lax.ppermute(value, axis, [(2 * o + q, 2 * (o + step) + q) for o in sourc...  38.8 us
    pallas_call x3, Pallas kernels, transpose_product(): pl.pallas_call(kernel, in_specs=[VMEM] * (len(pieces) + 1), out_specs=VME...  11.5 us
    pallas_call x2, Pallas kernels, weight_term(): pl.pallas_call(kernel, in_specs=[ANY] * len(operands), out_specs=[VMEM] *...  10.5 us
    unnamed x59, local copies, waits for them, and re-layouts  10.1 us
    ppermute x2, starting transfers between devices, advance(): self.flying = [lax.ppermute(send, self.axis, route)]  9.89 us
    ppermute x4, starting transfers between devices, swap_in_layers(): lax.ppermute(value, ('section', axis), [(k * count + i, k * count + (i ^...  9.48 us
    ppermute x3, waiting for transfers between devices, to_stand_in(): return lax.ppermute(own, 'section', [(helped, 0)])  8.6 us
  transfers between devices with their start and end apart: 31, of which 9 were waited for; matrix products, arithmetic and copies ran while one was open for 8% of the time, Pallas kernels for 21%

profile of v3, /device:TPU:0, one launch (start us, length us, event | category | flops | bytes accessed | tf_op | source)
XLA Modules:
  0.0 217.0 jit_solution(23109215887723544)
XLA Ops:
  3.2 5.0 %shard_map.94 = (bf16[1024,512]{1,0:T(8,128)(2,1)}, bf16[512,2304]{1,0:T(8,128)(2,1)}) custom-call(s32[1]{0:T(128)} %bitcast.side_ref, f32[1,2048]{1,0:T(1,128)} %gain_ref.3, bf16[512,2048]{1,0:T(8,128)(2,1)} %bitcast.55, bf16[512,3072]{1,0:T(8,128)(2,1)} %bitcast.43), custom_call_target="tpu_custom_call" | custom-call | flops 1 | bytes 1 | tf_op jit(solution)/shard_map/pallas_call | solution.py:178
  8.3 3.0 %collective-permute-start = (bf16[512,2304]{1,0:T(8,128)(2,1)}, bf16[512,2304]{1,0:T(8,128)(2,1)}, u32[]{:S(2)}, u32[]{:S(2)}) collective-permute-start(bf16[512,2304]{1,0:T(8,128)(2,1)} %get-tuple-element.104), channel_id=1, source_target_pairs={{0,1},{1,0},{2,3},{3,2},{4,5},{5,4},{6,7},{7,6},{8,9},{9,8},{10,11... | collective-permute-start | bytes 7077896 | tf_op jit(solution)/shard_map/ppermute | solution.py:22
  11.3 1.9 slice_bitcast_fusion
  13.2 1.8 slice_bitcast_fusion.2
  15.0 8.6 %collective-permute-done.2 = f32[2048]{0:T(1024)S(1)} collective-permute-done((f32[2048]{0:T(1024)}, f32[2048]{0:T(1024)S(1)}, u32[]{:S(2)}, u32[]{:S(2)}) %collective-permute-start.2) | collective-permute-done | bytes 8224 | tf_op jit(solution)/shard_map/ppermute | solution.py:421
  23.6 1.7 broadcast_select_fusion.shard_ref
  25.3 5.8 %collective-permute-start.3 = (bf16[256,3072]{1,0:T(8,128)(2,1)S(1)}, bf16[256,3072]{1,0:T(8,128)(2,1)}, u32[]{:S(2)}, u32[]{:S(2)}) collective-permute-start(bf16[256,3072]{1,0:T(8,128)(2,1)S(1)} %broadcast_select_fusion.shard_ref), channel_id=1, source_target_pairs={{0,2},{1,3},{2,4},{3,5},{4,6},{5,7},{8,10},{9,11},{10,12},{11,13},... | collective-permute-start | bytes 4718600 | tf_op jit(solution)/shard_map/ppermute | solution.py:26
  32.3 2.0 pad_maximum_fusion
  35.8 16.8 %collective-permute-done.3.refs_0_ = bf16[256,3072]{1,0:T(8,128)(2,1)} collective-permute-done((bf16[256,3072]{1,0:T(8,128)(2,1)S(1)}, bf16[256,3072]{1,0:T(8,128)(2,1)}, u32[]{:S(2)}, u32[]{:S(2)}) %collective-permute-start.3) | collective-permute-done | bytes 1572896 | tf_op jit(solution)/shard_map/ppermute | solution.py:26
  52.6 9.7 %collective-permute-done.4.refs_3_ = bf16[256,3072]{1,0:T(8,128)(2,1)} collective-permute-done((bf16[256,3072]{1,0:T(8,128)(2,1)S(1)}, bf16[256,3072]{1,0:T(8,128)(2,1)}, u32[]{:S(2)}, u32[]{:S(2)}) %collective-permute-start.4) | collective-permute-done | bytes 1572896 | tf_op jit(solution)/shard_map/ppermute | solution.py:26
  62.3 1.8 collective-permute-start.8
  66.8 1.5 collective-permute-start.5
  68.3 1.9 copy-done.3
  71.4 4.6 %shard_map.95 = (bf16[1024,512]{1,0:T(8,128)(2,1)S(1)}, bf16[1024,1280]{1,0:T(8,128)(2,1)S(1)}) custom-call(bf16[1024,512]{1,0:T(8,128)(2,1)S(1)} %copy-done.10, bf16[512,3072]{1,0:T(8,128)(2,1)S(1)} %bitcast.45, bf16[512,2304]{1,0:T(8,128)(2,1)} %collective-permute-done.got_any), custom_call_target="tpu_custom_call" | custom-call | flops 1 | bytes 1 | tf_op jit(solution)/shard_map/pallas_call | solution.py:359
  78.1 4.6 %collective-permute-start.7 = (bf16[256,1280]{1,0:T(8,128)(2,1)}, bf16[256,1280]{1,0:T(8,128)(2,1)S(1)}, u32[]{:S(2)}, u32[]{:S(2)}) collective-permute-start(bf16[256,1280]{1,0:T(8,128)(2,1)} %shard_map.96), channel_id=1, source_target_pairs={{0,2},{1,3},{6,4},{7,5},{8,10},{9,11},{14,12},{15,13},{16,18},{17,... | collective-permute-start | bytes 1966088 | tf_op jit(solution)/shard_map/ppermute | solution.py:81
  82.8 8.9 %collective-permute-done.9.refs_4_ = bf16[256,3072]{1,0:T(8,128)(2,1)} collective-permute-done((bf16[256,3072]{1,0:T(8,128)(2,1)}, bf16[256,3072]{1,0:T(8,128)(2,1)}, u32[]{:S(2)}, u32[]{:S(2)}) %collective-permute-start.9) | collective-permute-done | bytes 1572896 | tf_op jit(solution)/shard_map/ppermute | solution.py:26
  91.6 1.8 collective-permute-done.7.refs_0_.refs_1_
  94.7 4.3 %collective-permute-start.12 = (bf16[256,1280]{1,0:T(8,128)(2,1)S(1)}, bf16[256,1280]{1,0:T(8,128)(2,1)S(1)}, u32[]{:S(2)}, u32[]{:S(2)}) collective-permute-start(bf16[256,1280]{1,0:T(8,128)(2,1)S(1)} %get-tuple-element.128), channel_id=1, source_target_pairs={{0,2},{1,3},{2,4},{3,5},{8,10},{9,11},{10,12},{11,13},{16,18},{17,... | collective-permute-start | bytes 1966088 | tf_op jit(solution)/shard_map/ppermute | solution.py:26
  99.0 1.8 collective-permute-start.10
  102.2 2.7 %collective-permute-done.5.got_any = bf16[512,1792]{1,0:T(8,128)(2,1)} collective-permute-done((bf16[512,1792]{1,0:T(8,128)(2,1)}, bf16[512,1792]{1,0:T(8,128)(2,1)}, u32[]{:S(2)}, u32[]{:S(2)}) %collective-permute-start.5) | collective-permute-done | bytes 1835040 | tf_op jit(solution)/shard_map/ppermute | solution.py:22
  104.8 1.9 collective-permute-start.15
  109.1 5.9 %shard_map.101.term_any.refs_1_ = bf16[1024,1792]{1,0:T(8,128)(2,1)S(1)} custom-call(bf16[1024,512]{1,0:T(8,128)(2,1)S(1)} %copy-done.11, bf16[512,3072]{1,0:T(8,128)(2,1)S(1)} %bitcast.46, bf16[512,1792]{1,0:T(8,128)(2,1)} %collective-permute-done.5.got_any, bf16[1024,512]{1,0:T(8,128)(2,1)S(1)} %copy-done.15), custom_call_target="tpu_custom_call" | custom-call | flops 1 | bytes 1 | tf_op jit(solution)/shard_map/pallas_call | solution.py:359
  117.3 5.3 %collective-permute-start.14 = (bf16[256,1792]{1,0:T(8,128)(2,1)}, bf16[256,1792]{1,0:T(8,128)(2,1)S(1)}, u32[]{:S(2)}, u32[]{:S(2)}) collective-permute-start(bf16[256,1792]{1,0:T(8,128)(2,1)} %shard_map.102), channel_id=1, source_target_pairs={{0,2},{1,3},{6,4},{7,5},{8,10},{9,11},{14,12},{15,13},{16,18},{17,... | collective-permute-start | bytes 2752520 | tf_op jit(solution)/shard_map/ppermute | solution.py:81
  122.7 2.8 %slice_select_fusion.refs_1_ = bf16[256,3072]{1,0:T(8,128)(2,1)} fusion(bf16[256,7168]{1,0:T(8,128)(2,1)} %collective-permute-done.6, pred[]{:T(512)S(6)} %eq.6, bf16[1,512,3072]{2,1,0:T(8,128)(2,1)S(1)} %copy-done.22), kind=kLoop, calls=%fused_computation.3 | loop fusion | flops 786432 | bytes 4718593 | tf_op jit(solution)/shard_map/jit(_where)/select_n | solution.py:466
  126.3 3.4 %collective-permute-start.19 = (bf16[256,3072]{1,0:T(8,128)(2,1)}, bf16[256,3072]{1,0:T(8,128)(2,1)}, u32[]{:S(2)}, u32[]{:S(2)}) collective-permute-start(bf16[256,3072]{1,0:T(8,128)(2,1)} %slice_select_fusion.refs_1_), channel_id=1, source_target_pairs={{0,1},{1,0},{2,3},{3,2},{4,5},{5,4},{6,7},{7,6},{8,9},{9,8},{10,11... | collective-permute-start | bytes 4718600 | tf_op jit(solution)/shard_map/ppermute | solution.py:424
  133.5 5.2 %collective-permute-done.14.refs_0_.refs_1_ = bf16[256,1792]{1,0:T(8,128)(2,1)S(1)} collective-permute-done((bf16[256,1792]{1,0:T(8,128)(2,1)}, bf16[256,1792]{1,0:T(8,128)(2,1)S(1)}, u32[]{:S(2)}, u32[]{:S(2)}) %collective-permute-start.14) | collective-permute-done | bytes 917536 | tf_op jit(solution)/shard_map/ppermute | solution.py:81
  138.7 1.4 shard_map.103
  140.2 4.3 %collective-permute-start.20 = (bf16[256,1792]{1,0:T(8,128)(2,1)S(1)}, bf16[256,1792]{1,0:T(8,128)(2,1)S(1)}, u32[]{:S(2)}, u32[]{:S(2)}) collective-permute-start(bf16[256,1792]{1,0:T(8,128)(2,1)S(1)} %get-tuple-element.156), channel_id=1, source_target_pairs={{0,2},{1,3},{2,4},{3,5},{8,10},{9,11},{10,12},{11,13},{16,18},{17,... | collective-permute-start | bytes 2752520 | tf_op jit(solution)/shard_map/ppermute | solution.py:26
  145.2 12.7 %collective-permute-start.17 = (bf16[256,1280]{1,0:T(8,128)(2,1)S(1)}, bf16[256,1280]{1,0:T(8,128)(2,1)S(1)}, u32[]{:S(2)}, u32[]{:S(2)}) collective-permute-start(bf16[256,1280]{1,0:T(8,128)(2,1)S(1)} %get-tuple-element.153), channel_id=1, source_target_pairs={{0,2},{1,3},{2,4},{3,5},{4,6},{5,7},{8,10},{9,11},{10,12},{11,13},... | collective-permute-start | bytes 1966088 | tf_op jit(solution)/shard_map/ppermute | solution.py:26
  158.0 2.7 %shard_map.99.refs_2_.refs_1_ = bf16[1024,3072]{1,0:T(8,128)(2,1)S(1)} custom-call(s32[1]{0:T(128)} %bitcast.12.pair_ref, bf16[256,3072]{1,0:T(8,128)(2,1)S(1)} %copy-done.6, bf16[256,3072]{1,0:T(8,128)(2,1)} %collective-permute-done.3.refs_0_, bf16[256,3072]{1,0:T(8,128)(2,1)} %collective-permute-done.8.refs_1_, ...), custom_call_target="tpu_custom_call" | custom-call | flops 1 | bytes 1 | tf_op jit(solution)/shard_map/pallas_call | solution.py:136
  160.7 1.5 collective-permute-start.18
  162.3 4.8 %shard_map.100.mine_ref = f32[512,1024]{1,0:T(8,128)S(1)} custom-call(bf16[256,3072]{1,0:T(8,128)(2,1)S(1)} %copy-done.9, bf16[256,3072]{1,0:T(8,128)(2,1)} %slice_select_fusion.refs_1_, bf16[1024,3072]{1,0:T(8,128)(2,1)S(1)} %shard_map.99.refs_2_.refs_1_), custom_call_target="tpu_custom_call" | custom-call | flops 1 | bytes 1 | tf_op jit(solution)/shard_map/pallas_call | solution.py:237
  167.1 3.2 %shard_map.104 = bf16[256,1024]{1,0:T(8,128)(2,1)S(1)} custom-call(bf16[256,3072]{1,0:T(8,128)(2,1)} %collective-permute-done.15.refs_0_, bf16[1024,3072]{1,0:T(8,128)(2,1)S(1)} %shard_map.99.refs_2_.refs_1_), custom_call_target="tpu_custom_call" | custom-call | flops 1 | bytes 1 | tf_op jit(solution)/shard_map/pallas_call | solution.py:237
  171.1 1.4 shard_map.105
  172.6 3.4 %shard_map.106 = bf16[256,1024]{1,0:T(8,128)(2,1)S(1)} custom-call(bf16[256,3072]{1,0:T(8,128)(2,1)} %collective-permute-done.19.refs_0_, bf16[1024,3072]{1,0:T(8,128)(2,1)S(1)} %shard_map.99.refs_2_.refs_1_), custom_call_target="tpu_custom_call" | custom-call | flops 1 | bytes 1 | tf_op jit(solution)/shard_map/pallas_call | solution.py:237
  176.0 3.5 %collective-permute-start.23 = (bf16[256,1024]{1,0:T(8,128)(2,1)S(1)}, bf16[256,1024]{1,0:T(8,128)(2,1)S(1)}, u32[]{:S(2)}, u32[]{:S(2)}) collective-permute-start(bf16[256,1024]{1,0:T(8,128)(2,1)S(1)} %shard_map.106), channel_id=1, source_target_pairs={{0,1},{1,0},{2,3},{3,2},{4,5},{5,4},{6,7},{7,6},{8,9},{9,8},{10,11... | collective-permute-start | bytes 1572872 | tf_op jit(solution)/shard_map/ppermute | solution.py:424
  179.5 5.4 %collective-permute-start.25 = (bf16[256,1792]{1,0:T(8,128)(2,1)S(1)}, bf16[256,1792]{1,0:T(8,128)(2,1)S(1)}, u32[]{:S(2)}, u32[]{:S(2)}) collective-permute-start(bf16[256,1792]{1,0:T(8,128)(2,1)S(1)} %get-tuple-element.180), channel_id=1, source_target_pairs={{0,2},{1,3},{2,4},{3,5},{4,6},{5,7},{8,10},{9,11},{10,12},{11,13},... | collective-permute-start | bytes 2752520 | tf_op jit(solution)/shard_map/ppermute | solution.py:26
  186.3 1.8 slice_select_fusion.1
  188.1 2.2 %shard_map.107 = bf16[256,2048]{1,0:T(8,128)(2,1)} custom-call(s32[1]{0:T(128)} %bitcast.side_ref, f32[512,1024]{1,0:T(8,128)S(1)} %shard_map.100.mine_ref, bf16[256,1024]{1,0:T(8,128)(2,1)S(1)} %collective-permute-done.16.theirs_ref, bf16[256,2048]{1,0:T(8,128)(2,1)S(1)} %copy-done.13, bf16[256,2048]{1,0:T(8,128)(2,1)S(1)} %copy-done.12, ...), custom_call_target="tpu_custom_call" | custom-call | flops 1 | bytes 1 | tf_op jit(solution)/shard_map/pallas_call | solution.py:271
  191.6 2.2 %shard_map.108 = bf16[256,2048]{1,0:T(8,128)(2,1)} custom-call(s32[1]{0:T(128)} %bitcast.side_ref, f32[512,1024]{1,0:T(8,128)S(1)} %shard_map.100.mine_ref, bf16[256,1024]{1,0:T(8,128)(2,1)S(1)} %collective-permute-done.23.theirs_ref, bf16[256,2048]{1,0:T(8,128)(2,1)S(1)} %get-tuple-element.204.rows_ref, bf16[256,2048]{1,0:T(8,128)(2,1)S(1)} %get-tuple-element.203.resid_ref, ...), custom_call_target="tpu_custom_call" | custom-call | flops 1 | bytes 1 | tf_op jit(solution)/shard_map/pallas_call | solution.py:271
  193.8 3.0 %collective-permute-start.24 = (bf16[256,2048]{1,0:T(8,128)(2,1)}, bf16[256,2048]{1,0:T(8,128)(2,1)}, u32[]{:S(2)}, u32[]{:S(2)}) collective-permute-start(bf16[256,2048]{1,0:T(8,128)(2,1)} %shard_map.108), channel_id=1, source_target_pairs={{8,0},{0,8},{24,16},{9,1},{1,9},{25,17},{10,2},{2,10},{26,18},{11,... | collective-permute-start | bytes 3145736 | tf_op jit(solution)/shard_map/ppermute | solution.py:441
  196.9 3.4 %collective-permute-done.26.refs_5_ = bf16[256,1792]{1,0:T(8,128)(2,1)S(1)} collective-permute-done((bf16[256,1792]{1,0:T(8,128)(2,1)S(1)}, bf16[256,1792]{1,0:T(8,128)(2,1)S(1)}, u32[]{:S(2)}, u32[]{:S(2)}) %collective-permute-start.26) | collective-permute-done | bytes 917536 | tf_op jit(solution)/shard_map/ppermute | solution.py:26
  200.2 3.1 %shard_map.109 = (f32[256,3072]{1,0:T(8,128)}, f32[1,256]{1,0:T(1,128)S(1)}) custom-call(s32[1]{0:T(128)} %bitcast.12.pair_ref, bf16[256,3072]{1,0:T(8,128)(2,1)S(1)} %bitcast.48, bf16[1024,1280]{1,0:T(8,128)(2,1)S(1)} %get-tuple-element.115.term_any.refs_0_, bf16[1024,1792]{1,0:T(8,128)(2,1)S(1)} %copy-done.1, ...), custom_call_target="tpu_custom_call" | custom-call | flops 1 | bytes 1 | tf_op jit(solution)/shard_map/pallas_call | solution.py:313
  203.3 2.1 collective-permute-start.27
  205.4 1.5 collective-permute-done.27
  207.0 2.5 %collective-permute-start.28 = (f32[512]{0:T(512)S(1)}, f32[512]{0:T(512)S(1)}, u32[]{:S(2)}, u32[]{:S(2)}) collective-permute-start(f32[512]{0:T(512)S(1)} %maximum_select_fusion), channel_id=1, source_target_pairs={{0,2},{1,3},{2,4},{3,5},{4,6},{5,7},{6,0},{7,1},{8,10},{9,11},{10,... | collective-permute-start | bytes 6152 | tf_op jit(solution)/shard_map/ppermute | solution.py:503
  209.8 2.9 %collective-permute-start.30 = (f32[512]{0:T(512)S(1)}, f32[512]{0:T(512)S(1)}, u32[]{:S(2)}, u32[]{:S(2)}) collective-permute-start(f32[512]{0:T(512)S(1)} %maximum_select_fusion), channel_id=1, source_target_pairs={{0,6},{1,7},{2,0},{3,1},{4,2},{5,3},{6,4},{7,5},{8,14},{9,15},{10,... | collective-permute-start | bytes 6152 | tf_op jit(solution)/shard_map/ppermute | solution.py:503
  212.7 3.1 %pad_maximum_fusion.1 = bf16[512,2048]{1,0:T(8,128)(2,1)} fusion(bf16[256,2048]{1,0:T(8,128)(2,1)} %collective-permute-done.24, bf16[256,2048]{1,0:T(8,128)(2,1)} %collective-permute-done.22), kind=kLoop, calls=%fused_computation.2 | loop fusion | flops 4194304 | bytes 4194304 | tf_op jit(solution)/shard_map/concatenate | solution.py:506
  (107 shorter events, 28.9 us)
Async XLA Ops:
  0.6 23.0 %collective-permute-start.1 = (bf16[256,3072]{1,0:T(8,128)(2,1)}, bf16[256,3072]{1,0:T(8,128)(2,1)}, u32[]{:S(2)}, u32[]{:S(2)}) collective-permute-start(bf16[256,3072]{1,0:T(8,128)(2,1)} %bitcast.47), channel_id=1, source_target_pairs={{16,0},{17,1},{18,2},{19,3},{20,4},{21,5},{22,6},{23,7}} | collective-permute-start | bytes 4718600 | tf_op jit(solution)/shard_map/ppermute | solution.py:421
  1.9 21.7 %collective-permute-start.2 = (f32[2048]{0:T(1024)}, f32[2048]{0:T(1024)S(1)}, u32[]{:S(2)}, u32[]{:S(2)}) collective-permute-start(f32[2048]{0:T(1024)} %bitcast.49), channel_id=1, source_target_pairs={{16,0},{17,1},{18,2},{19,3},{20,4},{21,5},{22,6},{23,7}} | collective-permute-start | bytes 24584 | tf_op jit(solution)/shard_map/ppermute | solution.py:421
  3.2 8.1 %copy-start.21 = (bf16[1,512,3072]{2,1,0:T(8,128)(2,1)S(1)}, bf16[1,512,3072]{2,1,0:T(8,128)(2,1)}, u32[]{:S(2)}) copy-start(bf16[1,512,3072]{2,1,0:T(8,128)(2,1)} %param.9) | copy-start | bytes 9437188
  8.3 4.9 %copy-start.24 = (bf16[1,512,2048]{2,1,0:T(8,128)(2,1)S(1)}, bf16[1,512,2048]{2,1,0:T(8,128)(2,1)}, u32[]{:S(2)}) copy-start(bf16[1,512,2048]{2,1,0:T(8,128)(2,1)} %param.8) | copy-start | bytes 6291460
  8.3 60.0 %collective-permute-start = (bf16[512,2304]{1,0:T(8,128)(2,1)}, bf16[512,2304]{1,0:T(8,128)(2,1)}, u32[]{:S(2)}, u32[]{:S(2)}) collective-permute-start(bf16[512,2304]{1,0:T(8,128)(2,1)} %get-tuple-element.104), channel_id=1, source_target_pairs={{0,1},{1,0},{2,3},{3,2},{4,5},{5,4},{6,7},{7,6},{8,9},{9,8},{10,11... | collective-permute-start | bytes 7077896 | tf_op jit(solution)/shard_map/ppermute | solution.py:22
  13.2 10.4 %copy-start.7 = (bf16[1,256,3072]{2,1,0:T(8,128)(2,1)S(1)}, bf16[1,256,3072]{2,1,0:T(8,128)(2,1)}, u32[]{:S(2)}) copy-start(bf16[1,256,3072]{2,1,0:T(8,128)(2,1)} %param.12) | copy-start | bytes 4718596
  15.0 17.3 %copy-start.23 = (bf16[256,3072]{1,0:T(8,128)(2,1)S(1)}, bf16[256,3072]{1,0:T(8,128)(2,1)}, u32[]{:S(2)}) copy-start(bf16[256,3072]{1,0:T(8,128)(2,1)} %get-tuple-element.205) | copy-start | bytes 4718596
  15.0 17.3 %copy-start.28 = (bf16[256,2048]{1,0:T(8,128)(2,1)S(1)}, bf16[256,2048]{1,0:T(8,128)(2,1)}, u32[]{:S(2)}) copy-start(bf16[256,2048]{1,0:T(8,128)(2,1)} %get-tuple-element.211) | copy-start | bytes 3145732
  25.3 9.1 %copy-start.5 = (bf16[256,3072]{1,0:T(8,128)(2,1)}, bf16[256,3072]{1,0:T(8,128)(2,1)S(1)}, u32[]{:S(2)}) copy-start(bf16[256,3072]{1,0:T(8,128)(2,1)S(1)} %broadcast_select_fusion.shard_ref) | copy-start | bytes 4718596
  25.3 27.3 %collective-permute-start.3 = (bf16[256,3072]{1,0:T(8,128)(2,1)S(1)}, bf16[256,3072]{1,0:T(8,128)(2,1)}, u32[]{:S(2)}, u32[]{:S(2)}) collective-permute-start(bf16[256,3072]{1,0:T(8,128)(2,1)S(1)} %broadcast_select_fusion.shard_ref), channel_id=1, source_target_pairs={{0,2},{1,3},{2,4},{3,5},{4,6},{5,7},{8,10},{9,11},{10,12},{11,13},... | collective-permute-start | bytes 4718600 | tf_op jit(solution)/shard_map/ppermute | solution.py:26
  31.0 31.3 %collective-permute-start.4 = (bf16[256,3072]{1,0:T(8,128)(2,1)S(1)}, bf16[256,3072]{1,0:T(8,128)(2,1)}, u32[]{:S(2)}, u32[]{:S(2)}) collective-permute-start(bf16[256,3072]{1,0:T(8,128)(2,1)S(1)} %broadcast_select_fusion.shard_ref), channel_id=1, source_target_pairs={{2,0},{3,1},{4,2},{5,3},{6,4},{7,5},{10,8},{11,9},{12,10},{13,11},... | collective-permute-start | bytes 4718600 | tf_op jit(solution)/shard_map/ppermute | solution.py:26
  32.3 33.1 %copy-start.2 = (bf16[1,512,3072]{2,1,0:T(8,128)(2,1)S(1)}, bf16[1,512,3072]{2,1,0:T(8,128)(2,1)}, u32[]{:S(2)}) copy-start(bf16[1,512,3072]{2,1,0:T(8,128)(2,1)} %param.11) | copy-start | bytes 9437188
  34.4 72.3 %collective-permute-start.6 = (bf16[256,7168]{1,0:T(8,128)(2,1)}, bf16[256,7168]{1,0:T(8,128)(2,1)}, u32[]{:S(2)}, u32[]{:S(2)}) collective-permute-start(bf16[256,7168]{1,0:T(8,128)(2,1)} %pad_maximum_fusion), channel_id=1, source_target_pairs={{16,0},{17,1},{18,2},{19,3},{20,4},{21,5},{22,6},{23,7}} | collective-permute-start | bytes 11010056 | tf_op jit(solution)/shard_map/ppermute | solution.py:421
  62.3 20.4 %collective-permute-start.8 = (bf16[256,3072]{1,0:T(8,128)(2,1)}, bf16[256,3072]{1,0:T(8,128)(2,1)}, u32[]{:S(2)}, u32[]{:S(2)}) collective-permute-start(bf16[256,3072]{1,0:T(8,128)(2,1)} %collective-permute-done.3.refs_0_), channel_id=1, source_target_pairs={{2,4},{3,5},{4,6},{5,7},{10,12},{11,13},{12,14},{13,15},{18,20},{1... | collective-permute-start | bytes 4718600 | tf_op jit(solution)/shard_map/ppermute | solution.py:26
  64.1 27.5 %collective-permute-start.9 = (bf16[256,3072]{1,0:T(8,128)(2,1)}, bf16[256,3072]{1,0:T(8,128)(2,1)}, u32[]{:S(2)}, u32[]{:S(2)}) collective-permute-start(bf16[256,3072]{1,0:T(8,128)(2,1)} %collective-permute-done.4.refs_3_), channel_id=1, source_target_pairs={{2,0},{3,1},{4,2},{5,3},{10,8},{11,9},{12,10},{13,11},{18,16},{19,... | collective-permute-start | bytes 4718600 | tf_op jit(solution)/shard_map/ppermute | solution.py:26
  66.8 38.0 %collective-permute-start.5 = (bf16[512,1792]{1,0:T(8,128)(2,1)}, bf16[512,1792]{1,0:T(8,128)(2,1)}, u32[]{:S(2)}, u32[]{:S(2)}) collective-permute-start(bf16[512,1792]{1,0:T(8,128)(2,1)} %slice.50), channel_id=1, source_target_pairs={{0,1},{1,0},{2,3},{3,2},{4,5},{5,4},{6,7},{7,6},{8,9},{9,8},{10,11... | collective-permute-start | bytes 5505032 | tf_op jit(solution)/shard_map/ppermute | solution.py:22
  78.1 15.4 %collective-permute-start.7 = (bf16[256,1280]{1,0:T(8,128)(2,1)}, bf16[256,1280]{1,0:T(8,128)(2,1)S(1)}, u32[]{:S(2)}, u32[]{:S(2)}) collective-permute-start(bf16[256,1280]{1,0:T(8,128)(2,1)} %shard_map.96), channel_id=1, source_target_pairs={{0,2},{1,3},{6,4},{7,5},{8,10},{9,11},{14,12},{15,13},{16,18},{17,... | collective-permute-start | bytes 1966088 | tf_op jit(solution)/shard_map/ppermute | solution.py:81
  82.7 24.0 %copy-start.4 = (bf16[1,512,3072]{2,1,0:T(8,128)(2,1)S(1)}, bf16[1,512,3072]{2,1,0:T(8,128)(2,1)}, u32[]{:S(2)}) copy-start(bf16[1,512,3072]{2,1,0:T(8,128)(2,1)} %param.11) | copy-start | bytes 9437188
  94.7 22.6 %collective-permute-start.12 = (bf16[256,1280]{1,0:T(8,128)(2,1)S(1)}, bf16[256,1280]{1,0:T(8,128)(2,1)S(1)}, u32[]{:S(2)}, u32[]{:S(2)}) collective-permute-start(bf16[256,1280]{1,0:T(8,128)(2,1)S(1)} %get-tuple-element.128), channel_id=1, source_target_pairs={{0,2},{1,3},{2,4},{3,5},{8,10},{9,11},{10,12},{11,13},{16,18},{17,... | collective-permute-start | bytes 1966088 | tf_op jit(solution)/shard_map/ppermute | solution.py:26
  99.0 34.4 %collective-permute-start.10 = (bf16[256,3072]{1,0:T(8,128)(2,1)}, bf16[256,3072]{1,0:T(8,128)(2,1)}, u32[]{:S(2)}, u32[]{:S(2)}) collective-permute-start(bf16[256,3072]{1,0:T(8,128)(2,1)} %collective-permute-done.8.refs_1_), channel_id=1, source_target_pairs={{4,6},{5,7},{12,14},{13,15},{20,22},{21,23},{28,30},{29,31}} | collective-permute-start | bytes 4718600 | tf_op jit(solution)/shard_map/ppermute | solution.py:26
  100.9 32.6 %collective-permute-start.11 = (bf16[256,3072]{1,0:T(8,128)(2,1)}, bf16[256,3072]{1,0:T(8,128)(2,1)}, u32[]{:S(2)}, u32[]{:S(2)}) collective-permute-start(bf16[256,3072]{1,0:T(8,128)(2,1)} %collective-permute-done.9.refs_4_), channel_id=1, source_target_pairs={{2,0},{3,1},{10,8},{11,9},{18,16},{19,17},{26,24},{27,25}} | collective-permute-start | bytes 4718600 | tf_op jit(solution)/shard_map/ppermute | solution.py:26
  104.8 55.9 %collective-permute-start.15 = (bf16[256,3072]{1,0:T(8,128)(2,1)}, bf16[256,3072]{1,0:T(8,128)(2,1)}, u32[]{:S(2)}, u32[]{:S(2)}) collective-permute-start(bf16[256,3072]{1,0:T(8,128)(2,1)} %get-tuple-element.111.refs_0_), channel_id=1, source_target_pairs={{8,9},{9,8},{10,11},{11,10},{12,13},{13,12},{14,15},{15,14},{16,17... | collective-permute-start | bytes 4718600 | tf_op jit(solution)/shard_map/ppermute | solution.py:424
  115.0 7.6 %copy-start.22 = (bf16[1,512,3072]{2,1,0:T(8,128)(2,1)S(1)}, bf16[1,512,3072]{2,1,0:T(8,128)(2,1)}, u32[]{:S(2)}) copy-start(bf16[1,512,3072]{2,1,0:T(8,128)(2,1)} %param.9) | copy-start | bytes 9437188
  115.0 10.5 %collective-permute-start.13 = (bf16[256,1280]{1,0:T(8,128)(2,1)S(1)}, bf16[256,1280]{1,0:T(8,128)(2,1)S(1)}, u32[]{:S(2)}, u32[]{:S(2)}) collective-permute-start(bf16[256,1280]{1,0:T(8,128)(2,1)S(1)} %get-tuple-element.129), channel_id=1, source_target_pairs={{4,2},{5,3},{6,4},{7,5},{12,10},{13,11},{14,12},{15,13},{20,18},{2... | collective-permute-start | bytes 1966088 | tf_op jit(solution)/shard_map/ppermute | solution.py:26
  117.3 8.1 %copy-start.16 = (bf16[256,1280]{1,0:T(8,128)(2,1)}, bf16[256,1280]{1,0:T(8,128)(2,1)S(1)}, u32[]{:S(2)}) copy-start(bf16[256,1280]{1,0:T(8,128)(2,1)S(1)} %collective-permute-done.12.refs_0_) | copy-start | bytes 1966084
  117.3 21.4 %collective-permute-start.14 = (bf16[256,1792]{1,0:T(8,128)(2,1)}, bf16[256,1792]{1,0:T(8,128)(2,1)S(1)}, u32[]{:S(2)}, u32[]{:S(2)}) collective-permute-start(bf16[256,1792]{1,0:T(8,128)(2,1)} %shard_map.102), channel_id=1, source_target_pairs={{0,2},{1,3},{6,4},{7,5},{8,10},{9,11},{14,12},{15,13},{16,18},{17,... | collective-permute-start | bytes 2752520 | tf_op jit(solution)/shard_map/ppermute | solution.py:81
  126.3 46.2 %collective-permute-start.19 = (bf16[256,3072]{1,0:T(8,128)(2,1)}, bf16[256,3072]{1,0:T(8,128)(2,1)}, u32[]{:S(2)}, u32[]{:S(2)}) collective-permute-start(bf16[256,3072]{1,0:T(8,128)(2,1)} %slice_select_fusion.refs_1_), channel_id=1, source_target_pairs={{0,1},{1,0},{2,3},{3,2},{4,5},{5,4},{6,7},{7,6},{8,9},{9,8},{10,11... | collective-permute-start | bytes 4718600 | tf_op jit(solution)/shard_map/ppermute | solution.py:424
  129.7 9.0 %copy-start.1 = (bf16[1024,1792]{1,0:T(8,128)(2,1)S(1)}, bf16[1024,1792]{1,0:T(8,128)(2,1)}, u32[]{:S(2)}) copy-start(bf16[1024,1792]{1,0:T(8,128)(2,1)} %copy-done) | copy-start | bytes 11010052
  133.4 24.5 %copy-start.6 = (bf16[256,3072]{1,0:T(8,128)(2,1)S(1)}, bf16[256,3072]{1,0:T(8,128)(2,1)}, u32[]{:S(2)}) copy-start(bf16[256,3072]{1,0:T(8,128)(2,1)} %copy-done.5) | copy-start | bytes 4718596
  140.2 30.2 %collective-permute-start.20 = (bf16[256,1792]{1,0:T(8,128)(2,1)S(1)}, bf16[256,1792]{1,0:T(8,128)(2,1)S(1)}, u32[]{:S(2)}, u32[]{:S(2)}) collective-permute-start(bf16[256,1792]{1,0:T(8,128)(2,1)S(1)} %get-tuple-element.156), channel_id=1, source_target_pairs={{0,2},{1,3},{2,4},{3,5},{8,10},{9,11},{10,12},{11,13},{16,18},{17,... | collective-permute-start | bytes 2752520 | tf_op jit(solution)/shard_map/ppermute | solution.py:26
  144.5 26.6 %collective-permute-start.21 = (bf16[256,1792]{1,0:T(8,128)(2,1)S(1)}, bf16[256,1792]{1,0:T(8,128)(2,1)S(1)}, u32[]{:S(2)}, u32[]{:S(2)}) collective-permute-start(bf16[256,1792]{1,0:T(8,128)(2,1)S(1)} %get-tuple-element.157), channel_id=1, source_target_pairs={{4,2},{5,3},{6,4},{7,5},{12,10},{13,11},{14,12},{15,13},{20,18},{2... | collective-permute-start | bytes 2752520 | tf_op jit(solution)/shard_map/ppermute | solution.py:26
  145.2 39.7 %collective-permute-start.17 = (bf16[256,1280]{1,0:T(8,128)(2,1)S(1)}, bf16[256,1280]{1,0:T(8,128)(2,1)S(1)}, u32[]{:S(2)}, u32[]{:S(2)}) collective-permute-start(bf16[256,1280]{1,0:T(8,128)(2,1)S(1)} %get-tuple-element.153), channel_id=1, source_target_pairs={{0,2},{1,3},{2,4},{3,5},{4,6},{5,7},{8,10},{9,11},{10,12},{11,13},... | collective-permute-start | bytes 1966088 | tf_op jit(solution)/shard_map/ppermute | solution.py:26
  160.7 27.3 %collective-permute-start.18 = (bf16[256,1280]{1,0:T(8,128)(2,1)S(1)}, bf16[256,1280]{1,0:T(8,128)(2,1)S(1)}, u32[]{:S(2)}, u32[]{:S(2)}) collective-permute-start(bf16[256,1280]{1,0:T(8,128)(2,1)S(1)} %get-tuple-element.154), channel_id=1, source_target_pairs={{2,0},{3,1},{4,2},{5,3},{6,4},{7,5},{10,8},{11,9},{12,10},{13,11},... | collective-permute-start | bytes 1966088 | tf_op jit(solution)/shard_map/ppermute | solution.py:26
  170.4 17.7 %collective-permute-start.16 = (bf16[256,1024]{1,0:T(8,128)(2,1)S(1)}, bf16[256,1024]{1,0:T(8,128)(2,1)S(1)}, u32[]{:S(2)}, u32[]{:S(2)}) collective-permute-start(bf16[256,1024]{1,0:T(8,128)(2,1)S(1)} %shard_map.104), channel_id=1, source_target_pairs={{8,9},{9,8},{10,11},{11,10},{12,13},{13,12},{14,15},{15,14},{16,17... | collective-permute-start | bytes 1572872 | tf_op jit(solution)/shard_map/ppermute | solution.py:424
  172.5 13.7 %copy-start.25 = (bf16[1,512,2048]{2,1,0:T(8,128)(2,1)S(1)}, bf16[1,512,2048]{2,1,0:T(8,128)(2,1)}, u32[]{:S(2)}) copy-start(bf16[1,512,2048]{2,1,0:T(8,128)(2,1)} %param.8) | copy-start | bytes 6291460
  172.5 13.7 %copy-start.27 = (bf16[1,512,2048]{2,1,0:T(8,128)(2,1)S(1)}, bf16[1,512,2048]{2,1,0:T(8,128)(2,1)}, u32[]{:S(2)}) copy-start(bf16[1,512,2048]{2,1,0:T(8,128)(2,1)} %param.7) | copy-start | bytes 6291460
  175.9 12.1 %copy-start.12 = (bf16[256,2048]{1,0:T(8,128)(2,1)S(1)}, bf16[256,2048]{1,0:T(8,128)(2,1)}, u32[]{:S(2)}) copy-start(bf16[256,2048]{1,0:T(8,128)(2,1)} %get-tuple-element.207.resid_ref) | copy-start | bytes 3145732
  176.0 12.1 %copy-start.13 = (bf16[256,2048]{1,0:T(8,128)(2,1)S(1)}, bf16[256,2048]{1,0:T(8,128)(2,1)}, u32[]{:S(2)}) copy-start(bf16[256,2048]{1,0:T(8,128)(2,1)} %get-tuple-element.212.rows_ref) | copy-start | bytes 3145732
  176.0 15.6 %collective-permute-start.23 = (bf16[256,1024]{1,0:T(8,128)(2,1)S(1)}, bf16[256,1024]{1,0:T(8,128)(2,1)S(1)}, u32[]{:S(2)}, u32[]{:S(2)}) collective-permute-start(bf16[256,1024]{1,0:T(8,128)(2,1)S(1)} %shard_map.106), channel_id=1, source_target_pairs={{0,1},{1,0},{2,3},{3,2},{4,5},{5,4},{6,7},{7,6},{8,9},{9,8},{10,11... | collective-permute-start | bytes 1572872 | tf_op jit(solution)/shard_map/ppermute | solution.py:424
  179.5 17.3 %collective-permute-start.25 = (bf16[256,1792]{1,0:T(8,128)(2,1)S(1)}, bf16[256,1792]{1,0:T(8,128)(2,1)S(1)}, u32[]{:S(2)}, u32[]{:S(2)}) collective-permute-start(bf16[256,1792]{1,0:T(8,128)(2,1)S(1)} %get-tuple-element.180), channel_id=1, source_target_pairs={{0,2},{1,3},{2,4},{3,5},{4,6},{5,7},{8,10},{9,11},{10,12},{11,13},... | collective-permute-start | bytes 2752520 | tf_op jit(solution)/shard_map/ppermute | solution.py:26
  184.9 15.3 %collective-permute-start.26 = (bf16[256,1792]{1,0:T(8,128)(2,1)S(1)}, bf16[256,1792]{1,0:T(8,128)(2,1)S(1)}, u32[]{:S(2)}, u32[]{:S(2)}) collective-permute-start(bf16[256,1792]{1,0:T(8,128)(2,1)S(1)} %get-tuple-element.181), channel_id=1, source_target_pairs={{2,0},{3,1},{4,2},{5,3},{6,4},{7,5},{10,8},{11,9},{12,10},{13,11},... | collective-permute-start | bytes 2752520 | tf_op jit(solution)/shard_map/ppermute | solution.py:26
  190.3 22.4 %collective-permute-start.22 = (bf16[256,2048]{1,0:T(8,128)(2,1)}, bf16[256,2048]{1,0:T(8,128)(2,1)}, u32[]{:S(2)}, u32[]{:S(2)}) collective-permute-start(bf16[256,2048]{1,0:T(8,128)(2,1)} %shard_map.107), channel_id=1, source_target_pairs={{8,0},{16,8},{24,16},{9,1},{17,9},{25,17},{10,2},{18,10},{26,18},{... | collective-permute-start | bytes 3145736 | tf_op jit(solution)/shard_map/ppermute | solution.py:441
  191.6 8.7 %copy-start.8 = (bf16[1,256,3072]{2,1,0:T(8,128)(2,1)S(1)}, bf16[1,256,3072]{2,1,0:T(8,128)(2,1)}, u32[]{:S(2)}) copy-start(bf16[1,256,3072]{2,1,0:T(8,128)(2,1)} %param.12) | copy-start | bytes 4718596
  193.8 18.9 %collective-permute-start.24 = (bf16[256,2048]{1,0:T(8,128)(2,1)}, bf16[256,2048]{1,0:T(8,128)(2,1)}, u32[]{:S(2)}, u32[]{:S(2)}) collective-permute-start(bf16[256,2048]{1,0:T(8,128)(2,1)} %shard_map.108), channel_id=1, source_target_pairs={{8,0},{0,8},{24,16},{9,1},{1,9},{25,17},{10,2},{2,10},{26,18},{11,... | collective-permute-start | bytes 3145736 | tf_op jit(solution)/shard_map/ppermute | solution.py:441
  203.3 3.6 %collective-permute-start.27 = (f32[256]{0:T(256)S(1)}, f32[256]{0:T(256)S(1)}, u32[]{:S(2)}, u32[]{:S(2)}) collective-permute-start(f32[256]{0:T(256)S(1)} %bitcast.53), channel_id=1, source_target_pairs={{0,1},{1,0},{2,3},{3,2},{4,5},{5,4},{6,7},{7,6},{8,9},{9,8},{10,11... | collective-permute-start | bytes 3080 | tf_op jit(solution)/shard_map/ppermute | solution.py:22
  207.0 8.8 %collective-permute-start.28 = (f32[512]{0:T(512)S(1)}, f32[512]{0:T(512)S(1)}, u32[]{:S(2)}, u32[]{:S(2)}) collective-permute-start(f32[512]{0:T(512)S(1)} %maximum_select_fusion), channel_id=1, source_target_pairs={{0,2},{1,3},{2,4},{3,5},{4,6},{5,7},{6,0},{7,1},{8,10},{9,11},{10,... | collective-permute-start | bytes 6152 | tf_op jit(solution)/shard_map/ppermute | solution.py:503
  209.4 6.4 %collective-permute-start.29 = (f32[512]{0:T(512)S(1)}, f32[512]{0:T(512)S(1)}, u32[]{:S(2)}, u32[]{:S(2)}) collective-permute-start(f32[512]{0:T(512)S(1)} %maximum_select_fusion), channel_id=1, source_target_pairs={{0,4},{1,5},{2,6},{3,7},{4,0},{5,1},{6,2},{7,3},{8,12},{9,13},{10,... | collective-permute-start | bytes 6152 | tf_op jit(solution)/shard_map/ppermute | solution.py:503
  209.8 6.0 %collective-permute-start.30 = (f32[512]{0:T(512)S(1)}, f32[512]{0:T(512)S(1)}, u32[]{:S(2)}, u32[]{:S(2)}) collective-permute-start(f32[512]{0:T(512)S(1)} %maximum_select_fusion), channel_id=1, source_target_pairs={{0,6},{1,7},{2,0},{3,1},{4,2},{5,3},{6,4},{7,5},{8,14},{9,15},{10,... | collective-permute-start | bytes 6152 | tf_op jit(solution)/shard_map/ppermute | solution.py:503
  (12 other events, 25.5 us)
